TPU v7x, 128 devices: a whole 4x4x4 slice. The times are simulated.
128 devices in a mesh: gx: 16 (over z, y), gy: 8 (over x, core).
Axes of the slice: x: 4, y: 4, z: 4, core: 2. Of those that a mesh axis runs over, the one named last changes fastest.
Arguments:
- tracer: float32 [16, 20, 64, 2048], P(None, None, 'gy', 'gx'), may hold values from -6 to 6
- east_vel: float32 [20, 64, 2048], P(None, 'gy', 'gx'), may hold values from -0.5 to 0.5
- north_vel: float32 [20, 64, 2048], P(None, 'gy', 'gx'), may hold values from -0.5 to 0.5
- diffusion: float32 [20, 64, 2048], P(None, 'gy', 'gx'), may hold values from 0.01 to 0.1
- mixing: float32 [20, 64, 2048], P(None, 'gy', 'gx'), may hold values from 0.1 to 10
- level_count: int32 [64, 2048], P('gy', 'gx'), may hold values from 0 to 20, as said below
- fold_map: int32 [2048], replicated, may hold values from 0 to 2047, as said below
- surface_term: float32 [64, 2048], P('gy', 'gx'), may hold values from 0.02 to 0.2
Outputs:
- mixed: float32 [16, 20, 64, 2048], P(None, None, 'gy', 'gx')
- pressure: float32 [64, 2048], P('gy', 'gx')
- residual: float32 [64, 2048], P('gy', 'gx')
Inputs may be any that keep to these rules, and one draw needn't show every extreme that they name: level_count is each column's number of ocean levels; 0 marks land. fold_map[i] = (2 p - 1 - i) mod 2048 for one column p, so it is its own inverse and fixes no column.
All inputs are finite; a program needn't handle non-finite values.
Results may differ from a plain program's by a relative error of at most 0.0003.
Values sent between devices are 32-bit elements; how exact they have to be, the bound alone decides.
No kernel may reach another device: no remote copies, remote signals or barrier semaphores. Data moves between devices by JAX's collectives and lax.ppermute only.
A program may use at most 128 MiB of HBM per device.

v0:
```python
import jax
import jax.numpy as jnp
from jax import lax
from jax.sharding import PartitionSpec as P

ITERS = 4


NEIGHBOURS = [
    (0, 1, 1.0),
    (0, -1, 1.0),
    (1, 0, 1.0),
    (-1, 0, 1.0),
    (1, 1, 0.5),
    (1, -1, 0.5),
    (-1, 1, 0.5),
    (-1, -1, 0.5),
]


def extended(cells, sides, width):
    for axis, dim in sides:
        count = lax.axis_size(axis)
        head = lax.slice_in_dim(cells, 0, width, axis=dim)
        tail = lax.slice_in_dim(cells, cells.shape[dim] - width, cells.shape[dim], axis=dim)
        cells = jnp.concatenate(
            [
                lax.ppermute(tail, axis, [(i, (i + 1) % count) for i in range(count)]),
                cells,
                lax.ppermute(head, axis, [((i + 1) % count, i) for i in range(count)]),
            ],
            axis=dim,
        )
    return cells


def extend(field, fold_map):
    rows = field.shape[2]
    cols = field.shape[3]
    padded = extended(field, (("gx", 3), ("gy", 2)), 1)
    top_row = field[:, :, rows - 1, :]
    total_cols = fold_map.shape[0]
    whole_row = lax.all_gather(top_row, "gx", axis=2, tiled=True)
    start = lax.axis_index("gx") * cols
    wanted = (start - 1 + jnp.arange(cols + 2, dtype=jnp.int32)) % total_cols
    hits = wanted[:, None] == jnp.arange(total_cols, dtype=jnp.int32)[None, :]
    partner = jnp.sum(jnp.where(hits, fold_map[None, :], 0), axis=1)
    folded = jnp.take(whole_row, partner, axis=2)
    row_index = lax.axis_index("gy")
    upper = jnp.where(row_index == lax.axis_size("gy") - 1, folded, padded[:, :, rows + 1, :])
    lower = jnp.where(row_index == 0, 0.0, padded[:, :, 0, :])
    return jnp.concatenate(
        [lower[:, :, None, :], padded[:, :, 1 : rows + 1, :], upper[:, :, None, :]], axis=2
    )


def window(padded, row_off, col_off):
    rows = padded.shape[0] - 2
    cols = padded.shape[1] - 2
    return padded[1 + row_off : 1 + row_off + rows, 1 + col_off : 1 + col_off + cols]


def residual_energy(resid, scaled_now):
    return lax.psum(jnp.sum(resid * scaled_now), ("gx", "gy"))


def shards(tracer, east_vel, north_vel, diffusion, mixing, level_count, fold_map, surface_term):
    levels_count = mixing.shape[0]
    levels = jnp.arange(levels_count, dtype=jnp.int32)[:, None, None]
    level_mask = (levels < level_count[None]).astype(jnp.float32)
    masked = tracer * level_mask[None]
    padded = extend(masked, fold_map)
    east_side = padded[:, :, 1:-1, 2:]
    west_side = padded[:, :, 1:-1, :-2]
    north_side = padded[:, :, 2:, 1:-1]
    south_side = padded[:, :, :-2, 1:-1]
    explicit = masked + level_mask * (
        -0.5 * east_vel * (east_side - west_side)
        - 0.5 * north_vel * (north_side - south_side)
        + diffusion * (east_side + west_side + north_side + south_side - 4.0 * masked)
    )
    coupling = mixing * (levels + 1 < level_count[None]).astype(jnp.float32)
    c_prev = jnp.zeros_like(coupling[0])
    r_prev = jnp.zeros_like(explicit[:, 0])
    a_prev = jnp.zeros_like(coupling[0])
    c_list = []
    r_list = []
    for level in range(levels_count):
        a_now = coupling[level]
        lower = -a_prev
        denominator = 1.0 + a_prev + a_now - lower * c_prev
        c_now = -a_now / denominator
        r_now = (explicit[:, level] - lower * r_prev) / denominator
        c_list.append(c_now)
        r_list.append(r_now)
        c_prev, r_prev, a_prev = (c_now, r_now, a_now)
    x_next = jnp.zeros_like(explicit[:, 0])
    outs_list = [None] * levels_count
    for level in range(levels_count - 1, -1, -1):
        x_next = r_list[level] - c_list[level] * x_next
        outs_list[level] = x_next
    mixed = jnp.stack(outs_list, axis=1)
    thickness = (0.5 + 1.5 * jnp.arange(levels_count).astype(jnp.float32) / (levels_count - 1))[
        :, None, None
    ]
    depth = jnp.sum(thickness * level_mask, axis=0) / levels_count
    wet_cells = level_count > 0
    rhs = jnp.where(wet_cells, 0.25 * jnp.sum(thickness * (mixed[0] - mixed[1]), axis=0), 0.0)
    depth_pad = extend(depth[None, None], fold_map)[0, 0]
    couplings = [
        weight * jnp.minimum(depth, window(depth_pad, row_off, col_off))
        for row_off, col_off, weight in NEIGHBOURS
    ]
    total = jnp.zeros_like(depth)
    for entry in couplings:
        total = total + entry
    diag = jnp.where(wet_cells, surface_term + total, 1.0)
    pressure = jnp.zeros_like(rhs)
    residual = rhs
    scaled = residual / diag
    direction = scaled
    energy = residual_energy(residual, scaled)
    for step in range(ITERS):
        field_pad = extend(direction[None, None], fold_map)[0, 0]
        summed = jnp.zeros_like(direction)
        for apply_entry, (apply_row_off, apply_col_off, apply_weight) in zip(couplings, NEIGHBOURS):
            summed = summed + apply_entry * window(field_pad, apply_row_off, apply_col_off)
        image = jnp.where(wet_cells, diag * direction - summed, direction)
        step_size = energy / lax.psum(jnp.sum(direction * image), ("gx", "gy"))
        pressure = pressure + step_size * direction
        residual = residual - step_size * image
        if step + 1 < ITERS:
            scaled = residual / diag
            energy_new = residual_energy(residual, scaled)
            direction = scaled + energy_new / energy * direction
            energy = energy_new
    return (mixed, pressure, residual)


def solution(mesh):
    in_specs = (
        P(None, None, "gy", "gx"),
        P(None, "gy", "gx"),
        P(None, "gy", "gx"),
        P(None, "gy", "gx"),
        P(None, "gy", "gx"),
        P("gy", "gx"),
        P(),
        P("gy", "gx"),
    )
    out_specs = (P(None, None, "gy", "gx"), P("gy", "gx"), P("gy", "gx"))
    return jax.shard_map(shards, mesh=mesh, in_specs=in_specs, out_specs=out_specs, check_vma=False)
```

profile of v0, /device:TPU:1, one launch (start us, length us, event | category | flops | bytes accessed | tf_op | source)
XLA Modules:
  0.0 732.3 jit_solution(10540496201195540255)
XLA Ops:
  13.9 7.1 collective-permute-start
  44.0 18.9 %all-gather.8.cloned.1.call-done = f32[16,20,1,2048]{3,0,2,1:T(8,128)} async-done(((f32[16,20,1,128]{3,0,2,1:T(8,128)}), f32[16,20,1,2048]{3,0,2,1:T(8,128)}) %all-gather.8.cloned.1.call-update) | async-done | bytes 2621456 | tf_op jit(solution)/shard_map/all_gather | solution.py:43
  62.9 12.5 %copy.407 = f32[16,20,2048]{1,0,2:T(8,128)} copy(f32[16,20,2048]{2,0,1:T(8,128)} %bitcast.172) | data formatting | bytes 5242880 | tf_op jit(solution)/shard_map/all_gather | solution.py:43
  75.4 7.6 %gather_fusion = f32[130,16,20]{2,1,0:T(8,128)} fusion(f32[16,20,2048]{1,0,2:T(8,128)} %copy.407, s32[1024]{0:T(1024)} %pad_clamp_fusion.1), kind=kCustom, calls=%fused_computation.5 | custom fusion | bytes 333320 | tf_op jit(solution)/shard_map/jit(_take)/gather | solution.py:48
  93.2 15.3 %all-gather.1 = f32[1,1,1,2048]{3,2,1,0:T(1,128)S(1)} all-gather(f32[1,1,1,128]{3,2,1,0:T(1,128)S(1)} %slice.406), channel_id=3, replica_groups=mesh['gx'=16,'gy'=8] {'gx'}, dimensions={3}, use_global_device_ids=true | all-gather | bytes 8704 | tf_op jit(solution)/shard_map/all_gather | solution.py:43
  115.9 8.6 %collective-permute-start.6 = (f32[1,1,1,130]{3,2,1,0:T(1,128)S(1)}, f32[1,1,1,130]{3,2,1,0:T(1,128)S(1)}, u32[]{:S(2)}, u32[]{:S(2)}) collective-permute-start(f32[1,1,1,130]{3,2,1,0:T(1,128)S(1)} %get-tuple-element.133), channel_id=1, source_target_pairs={{0,1},{1,2},{2,3},{3,4},{4,5},{5,6},{6,7},{7,0},{8,9},{9,10},{10,1... | collective-permute-start | bytes 1568 | tf_op jit(solution)/shard_map/ppermute | solution.py:28
  127.8 13.0 %all-gather.2 = f32[1,1,1,2048]{3,2,1,0:T(1,128)S(1)} all-gather(f32[1,1,1,128]{3,2,1,0:T(1,128)S(1)} %slice.419), channel_id=4, replica_groups=mesh['gx'=16,'gy'=8] {'gx'}, dimensions={3}, use_global_device_ids=true | all-gather | bytes 8704 | tf_op jit(solution)/shard_map/all_gather | solution.py:43
  145.0 4.6 collective-permute-done.8
  149.6 6.0 collective-permute-start.10
  159.4 65.5 %all-reduce = (f32[]{:T(128)}, f32[]{:T(128)}) all-reduce(f32[]{:T(128)} %get-tuple-element.11, f32[]{:T(128)} %get-tuple-element.10), channel_id=1, replica_groups=mesh['gx'=16,'gy'=8] {'gx','gy'}, use_global_device_ids=true, to_apply=%region_4.6 | all-reduce | flops 2 | bytes 16 | tf_op jit(solution)/shard_map/psum | solution.py:64
  226.9 63.8 %psum.58 = f32[]{:T(128)} all-reduce(f32[]{:T(128)} %get-tuple-element.28), channel_id=1, replica_groups=mesh['gx'=16,'gy'=8] {'gx','gy'}, use_global_device_ids=true, to_apply=%region_8.10 | all-reduce | flops 1 | bytes 8 | tf_op jit(solution)/shard_map/psum | solution.py:64
  292.1 13.8 %all-gather.3 = f32[1,1,1,2048]{3,2,1,0:T(1,128)S(1)} all-gather(f32[1,1,1,128]{3,2,1,0:T(1,128)S(1)} %slice.432), channel_id=5, replica_groups=mesh['gx'=16,'gy'=8] {'gx'}, dimensions={3}, use_global_device_ids=true | all-gather | bytes 8704 | tf_op jit(solution)/shard_map/all_gather | solution.py:43
  310.2 4.5 collective-permute-done.12
  314.8 7.7 %collective-permute-start.14 = (f32[1,1,1,130]{3,2,1,0:T(1,128)S(1)}, f32[1,1,1,130]{3,2,1,0:T(1,128)S(1)}, u32[]{:S(2)}, u32[]{:S(2)}) collective-permute-start(f32[1,1,1,130]{3,2,1,0:T(1,128)S(1)} %get-tuple-element.129), channel_id=1, source_target_pairs={{0,1},{1,2},{2,3},{3,4},{4,5},{5,6},{6,7},{7,0},{8,9},{9,10},{10,1... | collective-permute-start | bytes 1568 | tf_op jit(solution)/shard_map/ppermute | solution.py:28
  326.3 64.3 %psum.59 = f32[]{:T(128)} all-reduce(f32[]{:T(128)} %get-tuple-element.26), channel_id=1, replica_groups=mesh['gx'=16,'gy'=8] {'gx','gy'}, use_global_device_ids=true, to_apply=%region_10.12 | all-reduce | flops 1 | bytes 8 | tf_op jit(solution)/shard_map/psum | solution.py:129
  392.5 62.9 %psum.60 = f32[]{:T(128)} all-reduce(f32[]{:T(128)} %get-tuple-element.23), channel_id=1, replica_groups=mesh['gx'=16,'gy'=8] {'gx','gy'}, use_global_device_ids=true, to_apply=%region_12.14 | all-reduce | flops 1 | bytes 8 | tf_op jit(solution)/shard_map/psum | solution.py:64
  456.9 14.9 %all-gather.4 = f32[1,1,1,2048]{3,2,1,0:T(1,128)S(1)} all-gather(f32[1,1,1,128]{3,2,1,0:T(1,128)S(1)} %slice.445), channel_id=6, replica_groups=mesh['gx'=16,'gy'=8] {'gx'}, dimensions={3}, use_global_device_ids=true | all-gather | bytes 8704 | tf_op jit(solution)/shard_map/all_gather | solution.py:43
  480.6 6.3 collective-permute-start.18
  490.7 66.0 %psum.61 = f32[]{:T(128)} all-reduce(f32[]{:T(128)} %get-tuple-element.21), channel_id=1, replica_groups=mesh['gx'=16,'gy'=8] {'gx','gy'}, use_global_device_ids=true, to_apply=%region_14.16 | all-reduce | flops 1 | bytes 8 | tf_op jit(solution)/shard_map/psum | solution.py:129
  558.6 62.5 %psum.62 = f32[]{:T(128)} all-reduce(f32[]{:T(128)} %get-tuple-element.18), channel_id=1, replica_groups=mesh['gx'=16,'gy'=8] {'gx','gy'}, use_global_device_ids=true, to_apply=%region_16.18 | all-reduce | flops 1 | bytes 8 | tf_op jit(solution)/shard_map/psum | solution.py:64
  622.6 15.8 %all-gather.5 = f32[1,1,1,2048]{3,2,1,0:T(1,128)S(1)} all-gather(f32[1,1,1,128]{3,2,1,0:T(1,128)S(1)} %slice.458), channel_id=7, replica_groups=mesh['gx'=16,'gy'=8] {'gx'}, dimensions={3}, use_global_device_ids=true | all-gather | bytes 8704 | tf_op jit(solution)/shard_map/all_gather | solution.py:43
  642.7 4.8 collective-permute-done.20
  647.6 5.3 collective-permute-start.22
  656.6 66.3 %psum.63 = f32[]{:T(128)} all-reduce(f32[]{:T(128)} %get-tuple-element.16), channel_id=1, replica_groups=mesh['gx'=16,'gy'=8] {'gx','gy'}, use_global_device_ids=true, to_apply=%region_18.20 | all-reduce | flops 1 | bytes 8 | tf_op jit(solution)/shard_map/psum | solution.py:129
  (289 shorter events, 89.5 us)
Async XLA Ops:
  7.2 55.7 %all-gather.8.cloned.1.call-start = ((), (), s32[]{:S(2)}) async-start(), calls=%async_computation | async-start | bytes 2785280 | tf_op jit(solution)/shard_map/all_gather | solution.py:43
  13.9 15.7 %collective-permute-start = (f32[16,20,8,1]{1,2,3,0:T(8,128)S(1)}, f32[16,20,8,1]{1,2,3,0:T(8,128)S(1)}, u32[]{:S(2)}, u32[]{:S(2)}) collective-permute-start(f32[16,20,8,1]{1,2,3,0:T(8,128)S(1)} %copy.400), channel_id=1, source_target_pairs={{8,0},{16,8},{24,16},{32,24},{40,32},{48,40},{56,48},{64,56},{72,6... | collective-permute-start | bytes 30728 | tf_op jit(solution)/shard_map/ppermute | solution.py:30
  21.8 8.7 %collective-permute-start.1 = (f32[16,20,8,1]{1,2,3,0:T(8,128)S(1)}, f32[16,20,8,1]{1,2,3,0:T(8,128)S(1)}, u32[]{:S(2)}, u32[]{:S(2)}) collective-permute-start(f32[16,20,8,1]{1,2,3,0:T(8,128)S(1)} %copy.402), channel_id=1, source_target_pairs={{0,8},{8,16},{16,24},{24,32},{32,40},{40,48},{48,56},{56,64},{64,7... | collective-permute-start | bytes 30728 | tf_op jit(solution)/shard_map/ppermute | solution.py:28
  36.6 6.1 collective-permute-start.3
  41.2 43.5 %collective-permute-start.2 = (f32[16,20,1,130]{3,0,2,1:T(8,128)}, f32[16,20,1,130]{3,0,2,1:T(8,128)}, u32[]{:S(2)}, u32[]{:S(2)}) collective-permute-start(f32[16,20,1,130]{3,0,2,1:T(8,128)} %copy.410), channel_id=1, source_target_pairs={{1,0},{2,1},{3,2},{4,3},{5,4},{6,5},{7,6},{0,7},{9,8},{10,9},{11,1... | collective-permute-start | bytes 499208 | tf_op jit(solution)/shard_map/ppermute | solution.py:30
  108.6 2.9 collective-permute-start.5
  110.1 5.8 collective-permute-start.4
  115.9 9.3 %collective-permute-start.6 = (f32[1,1,1,130]{3,2,1,0:T(1,128)S(1)}, f32[1,1,1,130]{3,2,1,0:T(1,128)S(1)}, u32[]{:S(2)}, u32[]{:S(2)}) collective-permute-start(f32[1,1,1,130]{3,2,1,0:T(1,128)S(1)} %get-tuple-element.133), channel_id=1, source_target_pairs={{0,1},{1,2},{2,3},{3,4},{4,5},{5,6},{6,7},{7,0},{8,9},{9,10},{10,1... | collective-permute-start | bytes 1568 | tf_op jit(solution)/shard_map/ppermute | solution.py:28
  124.5 3.0 collective-permute-start.7
  143.8 5.8 collective-permute-start.8
  149.6 6.8 collective-permute-start.10
  155.7 3.0 collective-permute-start.11
  307.4 2.8 collective-permute-start.13
  308.9 5.8 collective-permute-start.12
  314.8 8.4 %collective-permute-start.14 = (f32[1,1,1,130]{3,2,1,0:T(1,128)S(1)}, f32[1,1,1,130]{3,2,1,0:T(1,128)S(1)}, u32[]{:S(2)}, u32[]{:S(2)}) collective-permute-start(f32[1,1,1,130]{3,2,1,0:T(1,128)S(1)} %get-tuple-element.129), channel_id=1, source_target_pairs={{0,1},{1,2},{2,3},{3,4},{4,5},{5,6},{6,7},{7,0},{8,9},{9,10},{10,1... | collective-permute-start | bytes 1568 | tf_op jit(solution)/shard_map/ppermute | solution.py:28
  322.5 3.0 collective-permute-start.15
  473.3 2.8 collective-permute-start.17
  474.8 5.8 collective-permute-start.16
  480.6 7.6 %collective-permute-start.18 = (f32[1,1,1,130]{3,2,1,0:T(1,128)S(1)}, f32[1,1,1,130]{3,2,1,0:T(1,128)S(1)}, u32[]{:S(2)}, u32[]{:S(2)}) collective-permute-start(f32[1,1,1,130]{3,2,1,0:T(1,128)S(1)} %get-tuple-element.127), channel_id=1, source_target_pairs={{0,1},{1,2},{2,3},{3,4},{4,5},{5,6},{6,7},{7,0},{8,9},{9,10},{10,1... | collective-permute-start | bytes 1568 | tf_op jit(solution)/shard_map/ppermute | solution.py:28
  487.0 3.0 collective-permute-start.19
  639.9 2.8 collective-permute-start.21
  641.7 5.8 collective-permute-start.20
  647.6 6.9 collective-permute-start.22
  652.9 3.0 collective-permute-start.23
  (68 other events, 444.9 us)
Sparse Core Ops, SparseCore 0:
  10.3 52.5 all-gather.7
where the time goes:
time: 734 us; the launch traced here: 732 us
  blocking collectives  524 us (71%)
  waiting for transfers between devices  60.7 us (8%)
  starting transfers between devices  53.3 us (7%)
  local copies, waits for them, and re-layouts  40.6 us (6%)
  other arithmetic  28.9 us (4%)
  between operations  24.7 us (3%)
    psum x4, blocking collectives, residual_energy(): return lax.psum(jnp.sum(resid * scaled_now), ('gx', 'gy'))  255 us
    psum x3, blocking collectives, shards(): step_size = energy / lax.psum(jnp.sum(direction * image), ('gx', 'gy'))  197 us
    all_gather x5, blocking collectives, extend(): whole_row = lax.all_gather(top_row, 'gx', axis=2, tiled=True)  72.8 us
    ppermute x12, starting transfers between devices, extended(): lax.ppermute(tail, axis, [(i, (i + 1) % count) for i in range(count)])  36.4 us
    ppermute x12, waiting for transfers between devices, extended(): lax.ppermute(tail, axis, [(i, (i + 1) % count) for i in range(count)])  27.4 us
    all_gather x1, waiting for transfers between devices, extend(): whole_row = lax.all_gather(top_row, 'gx', axis=2, tiled=True)  18.9 us
    ppermute x12, starting transfers between devices, extended(): lax.ppermute(head, axis, [((i + 1) % count, i) for i in range(count)])  16.9 us
    gather x7, local copies, waits for them, and re-layouts, extend(): folded = jnp.take(whole_row, partner, axis=2)  16.5 us
  transfers between devices with their start and end apart: 25, of which 21 were waited for; matrix products, arithmetic and copies ran while one was open for 6% of the time, Pallas kernels for 0%

commit v1 on v0

v1 whole, which is shorter than its diff:
```python
import functools

import jax
import jax.numpy as jnp
from jax import lax
from jax.experimental import pallas as pl
from jax.experimental.pallas import tpu as pltpu
from jax.sharding import PartitionSpec as P

ITERS = 4
TRACERS, LEVELS, ROWS, COLS = 16, 20, 8, 128
GROUP = 4
BOTH = ("gx", "gy")
VMEM_LIMIT = 40 * 1024 * 1024

COL_TRACER, COL_DEEP, COL_SIZE = 0, 32, 72
ROW_TRACER, ROW_EAST, ROW_WEST, ROW_DIFF, ROW_FIELD, ROW_COUNT, ROW_SURFACE, ROW_SIZE = 0, 320, 360, 400, 560, 880, 888, 896
DEEP_SIZE = ROW_SIZE - ROW_EAST
COUNT_LANE, SURFACE_LANE = 100, 105

SCALAR_BOUND, FIELD_BOUND = 1500.0, 1.0e5

NEIGHBOURS = [
    (0, 1, 1.0),
    (0, -1, 1.0),
    (1, 0, 1.0),
    (-1, 0, 1.0),
    (1, 1, 0.5),
    (1, -1, 0.5),
    (-1, 1, 0.5),
    (-1, -1, 0.5),
]


def params():
    return pltpu.CompilerParams(vmem_limit_bytes=VMEM_LIMIT)


def whole():
    return pl.BlockSpec(memory_space=pltpu.VMEM)


def lanes():
    return lax.broadcasted_iota(jnp.int32, (ROWS, COLS), 1)


def sublanes():
    return lax.broadcasted_iota(jnp.int32, (ROWS, COLS), 0)


def roll(tile, shift, axis):
    size = tile.shape[axis]
    shift = shift % size
    return tile if shift == 0 else pltpu.roll(tile, shift, axis)


def turned(tile):
    return jnp.take_along_axis(tile, ROWS - 1 - sublanes(), axis=0)


def thickness(level):
    return 0.5 + 1.5 * level / (LEVELS - 1)


def pack_columns(items, lane):
    west = jnp.zeros((ROWS, COLS), jnp.float32)
    east = jnp.zeros((ROWS, COLS), jnp.float32)
    for tile, width, first in items:
        here = (lane >= first) & (lane < first + width)
        west = jnp.where(here, roll(tile, first, 1), west)
        east = jnp.where(here, roll(tile, first + width, 1), east)
    return west, east


def columns_kernel(tracer, east_vel, north_vel, diffusion, mixing, count, surface, to_west, to_east):
    lane = lanes()
    levels = count[...]

    def put(row, items):
        west, east = pack_columns(items, lane)
        to_west[row : row + ROWS, :] = west
        to_east[row : row + ROWS, :] = east

    for group in range(TRACERS // GROUP):
        put(
            COL_TRACER + group * ROWS,
            [
                (jnp.where(k < levels, tracer[group * GROUP + t, k], 0.0), 1, t * LEVELS + k)
                for t in range(GROUP)
                for k in range(LEVELS)
            ],
        )
    difference = [(jnp.where(k < levels, tracer[0, k] - tracer[1, k], 0.0), 5, 5 * k) for k in range(LEVELS)]
    put(
        COL_DEEP,
        difference + [(levels.astype(jnp.float32), 5, COUNT_LANE), (surface[...], 4, SURFACE_LANE)],
    )
    for at, field in enumerate((east_vel, north_vel, diffusion, mixing)):
        put(COL_DEEP + (1 + at) * ROWS, [(field[k], 4, 4 * k) for k in range(LEVELS)])


def pack_rows(kind, out, tracer, fields, count, surface):
    edge = 0 if kind == "south" else ROWS - 1
    turn = turned if kind == "fold" else (lambda tile: tile)
    low = sublanes() < 4
    levels = count[...]
    per = 2 * LEVELS
    level_row = lax.broadcasted_iota(jnp.int32, (per, COLS), 0)
    level_row = jnp.where(level_row >= LEVELS, level_row - LEVELS, level_row)
    wet = level_row < jnp.broadcast_to(levels[edge : edge + 1, :], (per, COLS))
    for at in range(TRACERS * LEVELS // per):
        rows = tracer[pl.ds(edge + ROWS * per * at, per, stride=ROWS), :]
        out[ROW_TRACER + per * at : ROW_TRACER + per * (at + 1), :] = jnp.where(wet, rows, 0.0)
    for k in range(LEVELS):
        one, two = ROWS * k, ROWS * (LEVELS + k)
        tile = jnp.where(k < levels, tracer[one : one + ROWS, :] - tracer[two : two + ROWS, :], 0.0)
        out[ROW_DIFF + ROWS * k : ROW_DIFF + ROWS * (k + 1), :] = turn(tile)
    for at, field in enumerate(fields):
        for m in range(LEVELS // 2):
            first, second = turn(field[2 * m]), turn(field[2 * m + 1])
            if kind == "north":
                tile = jnp.where(low, roll(first, 4, 0), second)
            else:
                tile = jnp.where(low, first, roll(second, 4, 0))
            row = ROW_FIELD + ROWS * (at * (LEVELS // 2) + m)
            out[row : row + ROWS, :] = tile
    out[ROW_COUNT : ROW_COUNT + ROWS, :] = turn(levels.astype(jnp.float32))
    out[ROW_SURFACE : ROW_SURFACE + ROWS, :] = turn(surface[...])


def rows_kernel(tracer, east_vel, north_vel, diffusion, mixing, count, surface, near, far):
    here = lax.axis_index("gy")
    top = lax.axis_size("gy") - 1
    rest = (tracer, (east_vel, north_vel, diffusion, mixing), count, surface)

    @pl.when(here % 2 == 0)
    def _():
        pack_rows("north", near, *rest)
        pack_rows("south", far, *rest)

    @pl.when(here % 2 == 1)
    def _():
        pack_rows("south", near, *rest)

    @pl.when((here % 2 == 1) & (here != top))
    def _():
        pack_rows("north", far, *rest)

    @pl.when(here == top)
    def _():
        pack_rows("fold", far, *rest)


def corners_kernel(east, west, near_in, far_in, near, far):
    del near_in, far_in
    here = lax.axis_index("gy")
    top = lax.axis_size("gy") - 1
    half = ROW_WEST - ROW_EAST
    near[:half, :] = east[COL_DEEP:, :]
    near[half:, :] = west[COL_DEEP:, :]

    @pl.when(here != top)
    def _():
        far[:half, :] = east[COL_DEEP:, :]
        far[half:, :] = west[COL_DEEP:, :]

    @pl.when(here == top)
    def _():
        for row in range(0, half, ROWS):
            far[row : row + ROWS, :] = turned(east[COL_DEEP + row : COL_DEEP + row + ROWS, :])
            far[half + row : half + row + ROWS, :] = turned(west[COL_DEEP + row : COL_DEEP + row + ROWS, :])


def pole_of(fold_map):
    return (fold_map[0] + 1) % (COLS * lax.axis_size("gx"))


def fold_index(offset, lane):
    return (offset - 1 - lane) & (COLS - 1)


def unpack(east, west, first, width, lane):
    right = roll(east, -first, 1)
    left = roll(west, -width - first, 1)
    return jnp.where(lane < width, right, jnp.where(lane >= COLS - width, left, 0.0))


def east_of(one, two, lane):
    a, b = roll(one, -1, 1), roll(two, -1, 1)
    return jnp.where(lane == COLS - 1, b, a), jnp.where(lane == COLS - 1, a, b)


def west_of(one, two, lane):
    a, b = roll(one, 1, 1), roll(two, 1, 1)
    return jnp.where(lane == 0, b, a), jnp.where(lane == 0, a, b)


def krylov_kernel(
    fold_map, tracer, east_vel, north_vel, diffusion, mixing, count, surface, from_east, from_west, near, far, extra,
    vectors, diagonal, right_side, partial,
    north_buf, south_buf, other_buf, halo_main, halo_side, diff_main, diff_side, misc,
):
    here = lax.axis_index("gy")
    top = lax.axis_size("gy") - 1
    lane, sub = lanes(), sublanes()
    low = sub < 4
    pole = pole_of(fold_map)
    offset = pole & (COLS - 1)
    odd_block = (pole // COLS) % 2 == 1
    fields = (east_vel, north_vel, diffusion, mixing)

    def at(ref, row):
        return ref[row - ROW_EAST : row - ROW_EAST + ROWS, :]

    @pl.when(here % 2 == 0)
    def _():
        north_buf[...] = near[ROW_EAST:, :]
        south_buf[...] = far[ROW_EAST:, :]

    @pl.when(here % 2 == 1)
    def _():
        south_buf[...] = near[ROW_EAST:, :]

    @pl.when((here % 2 == 1) & ((here != top) | odd_block))
    def _():
        north_buf[...] = far[ROW_EAST:, :]
        other_buf[...] = extra[ROW_EAST:, :]

    @pl.when((here == top) & jnp.logical_not(odd_block))
    def _():
        north_buf[...] = extra[ROW_EAST:, :]
        other_buf[...] = far[ROW_EAST:, :]

    def north_field(ref, f, k):
        tile = at(ref, ROW_FIELD + ROWS * (f * (LEVELS // 2) + k // 2))
        return roll(tile, 4 * (k % 2), 0)

    def south_field(f, k):
        tile = at(south_buf, ROW_FIELD + ROWS * (f * (LEVELS // 2) + k // 2))
        return roll(tile, 4 * (1 - k % 2), 0)

    def side(ref, f, first, width):
        return unpack(at(ref, ROW_EAST + ROWS * f), at(ref, ROW_WEST + ROWS * f), first, width, lane)

    @pl.when(here != top)
    def _():
        for f in range(4):
            east = jnp.where(low, at(north_buf, ROW_EAST + ROWS * (1 + f)), at(south_buf, ROW_EAST + ROWS * (1 + f)))
            west = jnp.where(low, at(north_buf, ROW_WEST + ROWS * (1 + f)), at(south_buf, ROW_WEST + ROWS * (1 + f)))
            for k in range(LEVELS):
                halo_main[f, k] = jnp.where(low, north_field(north_buf, f, k), south_field(f, k))
                halo_side[f, k] = unpack(east, west, 4 * k, 4, lane)
        for k in range(LEVELS):
            diff_main[k] = at(north_buf, ROW_DIFF + ROWS * k)
            diff_side[k] = side(north_buf, 0, 5 * k, 5)
        misc[0] = at(north_buf, ROW_COUNT)
        misc[1] = side(north_buf, 0, COUNT_LANE, 5)
        misc[2] = at(north_buf, ROW_SURFACE)
        misc[3] = side(north_buf, 0, SURFACE_LANE, 4)

    @pl.when(here == top)
    def _():
        index = fold_index(offset, lane)

        def folded(a_main, a_side, b_main, b_side):
            a, b = jnp.take_along_axis(a_main, index, axis=1), jnp.take_along_axis(b_main, index, axis=1)
            c, d = jnp.take_along_axis(a_side, index, axis=1), jnp.take_along_axis(b_side, index, axis=1)
            first = jnp.where(lane >= offset, a, b)
            right = jnp.where(lane < offset, a, c)
            left = jnp.where(lane >= offset, b, d)
            return first, jnp.where(lane < COLS // 2, right, left)

        for f in range(4):
            sign = -1.0 if f < 2 else 1.0
            for k in range(LEVELS):
                one, two = folded(
                    north_field(north_buf, f, k),
                    side(north_buf, 1 + f, 4 * k, 4),
                    north_field(other_buf, f, k),
                    side(other_buf, 1 + f, 4 * k, 4),
                )
                halo_main[f, k] = jnp.where(low, sign * one, south_field(f, k))
                halo_side[f, k] = jnp.where(low, sign * two, side(south_buf, 1 + f, 4 * k, 4))
        for k in range(LEVELS):
            diff_main[k], diff_side[k] = folded(
                at(north_buf, ROW_DIFF + ROWS * k),
                side(north_buf, 0, 5 * k, 5),
                at(other_buf, ROW_DIFF + ROWS * k),
                side(other_buf, 0, 5 * k, 5),
            )
        misc[0], misc[1] = folded(
            at(north_buf, ROW_COUNT),
            side(north_buf, 0, COUNT_LANE, 5),
            at(other_buf, ROW_COUNT),
            side(other_buf, 0, COUNT_LANE, 5),
        )
        misc[2], misc[3] = folded(
            at(north_buf, ROW_SURFACE),
            side(north_buf, 0, SURFACE_LANE, 4),
            at(other_buf, ROW_SURFACE),
            side(other_buf, 0, SURFACE_LANE, 4),
        )

    def column(f):
        row = COL_DEEP + ROWS * f
        return from_east[row : row + ROWS, :], from_west[row : row + ROWS, :]

    def neighbours_across(own, north, south):
        up, up_n, up_s = roll(own, -1, 0), roll(north, -1, 0), roll(south, -1, 0)
        down, down_n, down_s = roll(own, 1, 0), roll(north, 1, 0), roll(south, 1, 0)
        return (
            jnp.where(sub == 7, up_n, up),
            jnp.where(low, up_n, jnp.where(sub == 7, up, up_s)),
            jnp.where(sub == 0, down_s, down),
            jnp.where(sub == 0, down, jnp.where(low, down_n, down_s)),
        )

    def halo(pair):
        return jnp.where(low, pair[0], pair[1])

    counts_own = (count[...].astype(jnp.float32), unpack(*column(0), COUNT_LANE, 5, lane))
    counts_north = (misc[0], misc[1])
    counts_south = (at(south_buf, ROW_COUNT), side(south_buf, 0, COUNT_LANE, 5))
    counts = (counts_own[0], counts_own[1], halo((counts_north[0], counts_south[0])), halo((counts_north[1], counts_south[1])))
    surfaces = (
        surface[...],
        unpack(*column(0), SURFACE_LANE, 4, lane),
        halo((misc[2], at(south_buf, ROW_SURFACE))),
        halo((misc[3], side(south_buf, 0, SURFACE_LANE, 4))),
    )

    zero = jnp.zeros((ROWS, COLS), jnp.float32)
    c_prev, r_prev, a_prev = [zero] * 4, [zero] * 4, [zero] * 4
    c_list, r_list = [], []
    for k in range(LEVELS):
        own = (jnp.where(k < counts[0], tracer[0, k] - tracer[1, k], 0.0), unpack(*column(0), 5 * k, 5, lane))
        north = (diff_main[k], diff_side[k])
        south = (at(south_buf, ROW_DIFF + ROWS * k), side(south_buf, 0, 5 * k, 5))
        halos = (halo((north[0], south[0])), halo((north[1], south[1])))
        centre = (own[0], own[1], halos[0], halos[1])
        easts = east_of(*own, lane) + east_of(*halos, lane)
        wests = west_of(*own, lane) + west_of(*halos, lane)
        first = neighbours_across(own[0], north[0], south[0])
        second = neighbours_across(own[1], north[1], south[1])
        norths = (first[0], second[0], first[1], second[1])
        souths = (first[2], second[2], first[3], second[3])
        values = [
            (field[k], unpack(*column(1 + f), 4 * k, 4, lane), halo_main[f, k], halo_side[f, k])
            for f, field in enumerate(fields)
        ]
        c_now, r_now, a_now = [], [], []
        for i in range(4):
            u, v, spread, mix = (value[i] for value in values)
            change = (
                -0.5 * u * (easts[i] - wests[i])
                - 0.5 * v * (norths[i] - souths[i])
                + spread * (easts[i] + wests[i] + norths[i] + souths[i] - 4.0 * centre[i])
            )
            explicit = centre[i] + jnp.where(k < counts[i], change, 0.0)
            a = jnp.where(k + 1 < counts[i], mix, 0.0)
            inverse = 1.0 / (1.0 + a_prev[i] + a + a_prev[i] * c_prev[i])
            c_now.append(-a * inverse)
            r_now.append((explicit + a_prev[i] * r_prev[i]) * inverse)
            a_now.append(a)
        c_prev, r_prev, a_prev = c_now, r_now, a_now
        c_list.append(c_now)
        r_list.append(r_now)
    total, x_next = [zero] * 4, [zero] * 4
    for k in range(LEVELS - 1, -1, -1):
        x_next = [r_list[k][i] - c_list[k][i] * x_next[i] for i in range(4)]
        total = [total[i] + thickness(k) * x_next[i] for i in range(4)]
    rhs = [jnp.where(counts[i] > 0, 0.25 * total[i], 0.0) for i in range(4)]

    def depth_of(levels):
        depth = zero
        for k in range(LEVELS):
            depth = depth + jnp.where(k < levels, thickness(k), 0.0)
        return depth / LEVELS

    own = tuple(depth_of(levels) for levels in counts_own)
    north = tuple(depth_of(levels) for levels in counts_north)
    south = tuple(depth_of(levels) for levels in counts_south)
    depths = (own[0], own[1], halo((north[0], south[0])), halo((north[1], south[1])))

    def rows_of(own, north, south):
        first = neighbours_across(own[0], north[0], south[0])
        second = neighbours_across(own[1], north[1], south[1])
        return (first[0], second[0], first[1], second[1]), (first[2], second[2], first[3], second[3])

    def coupled(others, weight):
        return [weight * jnp.minimum(depths[i], others[i]) for i in range(4)]

    own_e, north_e, south_e = (east_of(*pair, lane) for pair in (own, north, south))
    own_w, north_w, south_w = (west_of(*pair, lane) for pair in (own, north, south))
    halo_e = (halo((north_e[0], south_e[0])), halo((north_e[1], south_e[1])))
    halo_w = (halo((north_w[0], south_w[0])), halo((north_w[1], south_w[1])))
    mid = rows_of(own, north, south)
    mid_e = rows_of(own_e, north_e, south_e)
    mid_w = rows_of(own_w, north_w, south_w)
    couplings = [
        coupled(own_e + halo_e, 1.0),
        coupled(own_w + halo_w, 1.0),
        coupled(mid[0], 1.0),
        coupled(mid[1], 1.0),
        coupled(mid_e[0], 0.5),
        coupled(mid_w[0], 0.5),
        coupled(mid_e[1], 0.5),
        coupled(mid_w[1], 0.5),
    ]
    diag = [
        jnp.where(counts[i] > 0, surfaces[i] + sum(entry[i] for entry in couplings), 1.0) for i in range(4)
    ]
    inverse = [1.0 / diag[i] for i in range(4)]
    couplings = [[entry[i] * inverse[i] for i in range(4)] for entry in couplings]

    def shifted_rows(tiles):
        north, south = [None] * 4, [None] * 4
        for i in range(2):
            a, b = roll(tiles[i], -1, 0), roll(tiles[i + 2], -1, 0)
            north[i], north[i + 2] = jnp.where(sub == 7, b, a), jnp.where(sub == 7, a, b)
            a, b = roll(tiles[i], 1, 0), roll(tiles[i + 2], 1, 0)
            south[i], south[i + 2] = jnp.where(sub == 0, b, a), jnp.where(sub == 0, a, b)
        return north, south

    def spread_out(tiles):
        east = east_of(tiles[0], tiles[1], lane) + east_of(tiles[2], tiles[3], lane)
        west = west_of(tiles[0], tiles[1], lane) + west_of(tiles[2], tiles[3], lane)
        mid_n, mid_s = shifted_rows(tiles)
        east_n, east_s = shifted_rows(east)
        west_n, west_s = shifted_rows(west)
        around = (east, west, mid_n, mid_s, east_n, west_n, east_s, west_s)
        return [sum(entry[i] * values[i] for entry, values in zip(couplings, around)) for i in range(4)]

    found = [[rhs[i] * inverse[i] for i in range(4)]]
    found.append(spread_out(found[0]))
    for _ in range(2, ITERS + 1):
        ahead = spread_out(found[-1])
        found.append([2.0 * ahead[i] - found[-2][i] for i in range(4)])
    for j in range(ITERS + 1):
        vectors[j] = found[j][0]
    diagonal[...] = diag[0]
    right_side[...] = rhs[0]
    weighted = [diag[0] * found[j][0] for j in range(ITERS + 1)]
    sums = [weighted[j] * found[j][0] for j in range(ITERS + 1)]
    sums += [weighted[j] * found[j + 1][0] for j in range(ITERS)]
    row = jnp.zeros((1, COLS), jnp.float32)
    for j, entry in enumerate(sums):
        row = jnp.where(lane[:1, :] == j, jnp.sum(entry, keepdims=True), row)
    partial[...] = jnp.broadcast_to(row, partial.shape)


def combine_kernel(moments, vectors, diagonal, pressure, residual, good):
    size = ITERS + 1
    sums = jnp.sum(moments[...], axis=0, keepdims=True)

    def lane_of(j):
        return jnp.broadcast_to(sums[:, j : j + 1], (ROWS, COLS))

    even = [lane_of(j) for j in range(size)]
    odd = [lane_of(size + j) for j in range(ITERS)]
    mu = []
    for j in range(size):
        mu.append(even[0] if j == 0 else 2.0 * even[j] - even[0])
        if j < ITERS:
            mu.append(odd[0] if j == 0 else 2.0 * odd[j] - odd[0])

    def mass(i, j):
        return 0.5 * (mu[i + j] + mu[abs(i - j)])

    def stiffness(i, j):
        i, j = min(i, j), max(i, j)
        if j == 0:
            return mu[0] - mu[1]
        return mass(i, j) - 0.5 * (mass(i, j + 1) + mass(i, j - 1))

    def form(values, entry):
        out = None
        for i in range(len(values)):
            inner = values[i] * entry(i, i)
            for j in range(i + 1, len(values)):
                inner = inner + 2.0 * values[j] * entry(i, j)
            out = values[i] * inner if out is None else out + values[i] * inner
        return out

    def applied(values):
        out = [value for value in values] + [jnp.zeros_like(values[0])]
        out[1] = out[1] - values[0]
        for j in range(1, len(values)):
            out[j + 1] = out[j + 1] - 0.5 * values[j]
            out[j - 1] = out[j - 1] - 0.5 * values[j]
        return out

    def amplified(values, result):
        total = sum(jnp.abs(value) for value in values)
        return total * total * mu[0] / result

    scaled = [jnp.ones((ROWS, COLS), jnp.float32)]
    direction = list(scaled)
    solution_at = []
    energy = mu[0]
    worst = jnp.zeros((ROWS, COLS), jnp.float32)
    fine = energy > 0.0
    for step in range(ITERS):
        image = applied(direction)
        curvature = form(direction, stiffness)
        step_size = energy / curvature
        fine = fine & (amplified(direction, curvature) <= SCALAR_BOUND) & (curvature > 0.0)
        solution_at = [
            step_size * value + (solution_at[j] if j < len(solution_at) else 0.0) for j, value in enumerate(direction)
        ]
        scaled = [
            (scaled[j] if j < len(scaled) else 0.0) - step_size * value for j, value in enumerate(image)
        ]
        energy_new = form(scaled, mass)
        bound = SCALAR_BOUND if step + 1 < ITERS else FIELD_BOUND
        fine = fine & (amplified(scaled, energy_new) <= bound) & (energy_new > 0.0)
        if step + 1 < ITERS:
            ratio = energy_new / energy
            direction = [
                scaled[j] + (ratio * direction[j] if j < len(direction) else 0.0) for j in range(len(scaled))
            ]
            energy = energy_new
    del worst
    pressure[...] = sum(solution_at[j] * vectors[j] for j in range(len(solution_at)))
    residual[...] = diagonal[...] * sum(scaled[j] * vectors[j] for j in range(len(scaled)))
    good[0] = jnp.min(jnp.where(fine, 1, 0).astype(jnp.int32))


def tracers_kernel(
    fold_map, tracer, east_vel, north_vel, diffusion, mixing, count, from_east, from_west, near, far, extra,
    mixed,
    north_rows, south_rows, factors,
):
    here = lax.axis_index("gy")
    top = lax.axis_size("gy") - 1
    lane, sub = lanes(), sublanes()
    levels = count[...]
    group = pl.program_id(0)

    @pl.when(group == 0)
    def _():
        @pl.when(here % 2 == 0)
        def _():
            north_rows[...] = near[...]
            south_rows[...] = far[...]

        @pl.when(here % 2 == 1)
        def _():
            south_rows[...] = near[...]

        @pl.when((here % 2 == 1) & (here != top))
        def _():
            north_rows[...] = far[...]

        @pl.when(here == top)
        def _():
            pole = pole_of(fold_map)
            offset = pole & (COLS - 1)
            odd_block = (pole // COLS) % 2 == 1
            index = fold_index(offset, lane)
            from_far = (lane >= offset) == odd_block
            for row in range(0, TRACERS * LEVELS, ROWS):
                a = jnp.take_along_axis(far[row : row + ROWS, :], index, axis=1)
                b = jnp.take_along_axis(extra[row : row + ROWS, :], index, axis=1)
                north_rows[row : row + ROWS, :] = jnp.where(from_far, a, b)

        c_prev = jnp.zeros((ROWS, COLS), jnp.float32)
        a_prev = jnp.zeros((ROWS, COLS), jnp.float32)
        for k in range(LEVELS):
            wet = jnp.where(k < levels, 1.0, 0.0)
            u, v, spread = 0.5 * wet * east_vel[k], 0.5 * wet * north_vel[k], wet * diffusion[k]
            a = jnp.where(k + 1 < levels, mixing[k], 0.0)
            inverse = 1.0 / (1.0 + a_prev + a + a_prev * c_prev)
            c_prev = -a * inverse
            factors[0, k] = 1.0 - 4.0 * spread
            factors[1, k] = spread - u
            factors[2, k] = spread + u
            factors[3, k] = spread - v
            factors[4, k] = spread + v
            factors[5, k] = inverse
            factors[6, k] = a_prev
            factors[7, k] = c_prev
            a_prev = a

    row = pl.multiple_of(group * ROWS, ROWS)
    columns_east = from_east[pl.ds(row, ROWS), :]
    columns_west = from_west[pl.ds(row, ROWS), :]
    r_prev = [jnp.zeros((ROWS, COLS), jnp.float32)] * GROUP
    for k in range(LEVELS):
        centre, to_e, to_w, to_n, to_s, inverse, above = (factors[j, k] for j in range(7))
        wet = k < levels
        for t in range(GROUP):
            cell = jnp.where(wet, tracer[t, k], 0.0)
            at = t * LEVELS + k
            halo_row = group * (GROUP * LEVELS) + at
            east = jnp.where(lane == COLS - 1, roll(columns_east, -1 - at, 1), roll(cell, -1, 1))
            west = jnp.where(lane == 0, roll(columns_west, -at, 1), roll(cell, 1, 1))
            north = jnp.where(sub == ROWS - 1, north_rows[pl.ds(halo_row, 1), :], roll(cell, -1, 0))
            south = jnp.where(sub == 0, south_rows[pl.ds(halo_row, 1), :], roll(cell, 1, 0))
            explicit = centre * cell + to_e * east + to_w * west + to_n * north + to_s * south
            r_prev[t] = (explicit + above * r_prev[t]) * inverse
            mixed[t, k] = r_prev[t]
    x_next = r_prev
    for k in range(LEVELS - 2, -1, -1):
        below = factors[7, k]
        for t in range(GROUP):
            x_next[t] = mixed[t, k] - below * x_next[t]
            mixed[t, k] = x_next[t]


def extended(cells, sides, width):
    for axis, dim in sides:
        count = lax.axis_size(axis)
        head = lax.slice_in_dim(cells, 0, width, axis=dim)
        tail = lax.slice_in_dim(cells, cells.shape[dim] - width, cells.shape[dim], axis=dim)
        cells = jnp.concatenate(
            [
                lax.ppermute(tail, axis, [(i, (i + 1) % count) for i in range(count)]),
                cells,
                lax.ppermute(head, axis, [((i + 1) % count, i) for i in range(count)]),
            ],
            axis=dim,
        )
    return cells


def extend(field, fold_map):
    rows, cols = field.shape
    padded = extended(field, (("gx", 1), ("gy", 0)), 1)
    total_cols = fold_map.shape[0]
    whole_row = lax.all_gather(field[rows - 1, :], "gx", axis=0, tiled=True)
    start = lax.axis_index("gx") * cols
    wanted = (start - 1 + jnp.arange(cols + 2, dtype=jnp.int32)) % total_cols
    folded = jnp.take(whole_row, jnp.take(fold_map, wanted), axis=0)
    row_index = lax.axis_index("gy")
    upper = jnp.where(row_index == lax.axis_size("gy") - 1, folded, padded[rows + 1, :])
    lower = jnp.where(row_index == 0, 0.0, padded[0, :])
    return jnp.concatenate([lower[None, :], padded[1 : rows + 1, :], upper[None, :]], axis=0)


def window(padded, row_off, col_off):
    rows = padded.shape[0] - 2
    cols = padded.shape[1] - 2
    return padded[1 + row_off : 1 + row_off + rows, 1 + col_off : 1 + col_off + cols]


def total_of(value):
    return lax.psum(jnp.sum(value), BOTH)


def direct_gradients(rhs, level_count, fold_map, surface_term):
    levels = jnp.arange(LEVELS, dtype=jnp.int32)[:, None, None]
    level_mask = (levels < level_count[None]).astype(jnp.float32)
    thick = (0.5 + 1.5 * jnp.arange(LEVELS).astype(jnp.float32) / (LEVELS - 1))[:, None, None]
    depth = jnp.sum(thick * level_mask, axis=0) / LEVELS
    wet_cells = level_count > 0
    depth_pad = extend(depth, fold_map)
    couplings = [
        weight * jnp.minimum(depth, window(depth_pad, row_off, col_off)) for row_off, col_off, weight in NEIGHBOURS
    ]
    diag = jnp.where(wet_cells, surface_term + sum(couplings), 1.0)

    def step(_, state):
        pressure, residual, direction, energy = state
        field_pad = extend(direction, fold_map)
        summed = jnp.zeros_like(direction)
        for entry, (row_off, col_off, _weight) in zip(couplings, NEIGHBOURS):
            summed = summed + entry * window(field_pad, row_off, col_off)
        image = jnp.where(wet_cells, diag * direction - summed, direction)
        step_size = energy / total_of(direction * image)
        pressure = pressure + step_size * direction
        residual = residual - step_size * image
        scaled = residual / diag
        energy_new = total_of(residual * scaled)
        return pressure, residual, scaled + energy_new / energy * direction, energy_new

    scaled = rhs / diag
    state = (jnp.zeros_like(rhs), rhs, scaled, total_of(rhs * scaled))
    state = lax.fori_loop(0, ITERS, step, state)
    return state[0], state[1]


def shards(sizes, tracer, east_vel, north_vel, diffusion, mixing, level_count, fold_map, surface_term):
    nx, ny = sizes
    f32 = jnp.float32

    def device(x, y):
        return (x % nx) * ny + y

    def kernel(body, **rest):
        return pl.pallas_call(body, compiler_params=params(), **rest)

    def shape(*dims):
        return jax.ShapeDtypeStruct(dims, f32)

    fields = (east_vel, north_vel, diffusion, mixing)

    to_west, to_east = kernel(
        columns_kernel,
        out_shape=(shape(COL_SIZE, COLS), shape(COL_SIZE, COLS)),
        in_specs=[whole()] * 7,
        out_specs=(whole(), whole()),
        name="pack_columns",
    )(tracer, *fields, level_count, surface_term)
    from_east = lax.ppermute(to_west, BOTH, [(device(x + 1, y), device(x, y)) for x in range(nx) for y in range(ny)])
    from_west = lax.ppermute(to_east, BOTH, [(device(x - 1, y), device(x, y)) for x in range(nx) for y in range(ny)])

    flat = tracer.reshape(TRACERS * LEVELS * ROWS, COLS)
    near, far = kernel(
        rows_kernel,
        out_shape=(shape(ROW_SIZE, COLS), shape(ROW_SIZE, COLS)),
        in_specs=[whole()] * 7,
        out_specs=(whole(), whole()),
        cost_estimate=pl.CostEstimate(flops=1000000, bytes_accessed=4000000, transcendentals=0),
        name="pack_rows",
    )(flat, *fields, level_count, surface_term)

    corner = pl.BlockSpec((ROW_DIFF - ROW_EAST, COLS), lambda i: (ROW_EAST // (ROW_DIFF - ROW_EAST), 0))
    column = pl.BlockSpec((COL_SIZE, COLS), lambda i: (0, 0))
    near, far = kernel(
        corners_kernel,
        grid=(1,),
        out_shape=(shape(ROW_SIZE, COLS), shape(ROW_SIZE, COLS)),
        in_specs=[column, column, pl.BlockSpec(memory_space=pl.ANY), pl.BlockSpec(memory_space=pl.ANY)],
        out_specs=(corner, corner),
        input_output_aliases={2: 0, 3: 1},
        name="put_corners",
    )(from_east, from_west, near, far)

    near = lax.ppermute(near, BOTH, [(device(x, y ^ 1), device(x, y)) for x in range(nx) for y in range(ny)])
    inner = [
        (device(x, y + 1 if y % 2 else y - 1), device(x, y)) for x in range(nx) for y in range(1, ny - 1)
    ]

    def across(turn):
        return [(device(turn - x, ny - 1), device(x, ny - 1)) for x in range(nx)]

    def exchange(block, rows):
        turns = ((block - 1) % nx, block)
        even, odd = turns if turns[0] % 2 == 0 else turns[::-1]
        return lax.ppermute(rows, BOTH, inner + across(even)), lax.ppermute(rows, BOTH, across(odd))

    block = (pole_of(fold_map) // COLS) % nx
    far, extra = lax.switch(block, [functools.partial(exchange, i) for i in range(nx)], far)

    smem = pl.BlockSpec(memory_space=pltpu.SMEM)
    pair = pl.BlockSpec((2, LEVELS, ROWS, COLS), lambda i: (0, 0, 0, 0))

    def all_of(array):
        return pl.BlockSpec(array.shape, lambda i: (0,) * array.ndim)

    rest = (*fields, level_count, surface_term, from_east, from_west, near, far, extra)
    vectors, diagonal, rhs, partial = kernel(
        krylov_kernel,
        grid=(1,),
        out_shape=(shape(ITERS + 1, ROWS, COLS), shape(ROWS, COLS), shape(ROWS, COLS), shape(nx * ny, COLS)),
        in_specs=[smem, pair] + [all_of(array) for array in rest],
        out_specs=tuple(
            pl.BlockSpec(dims, lambda i, n=len(dims): (0,) * n)
            for dims in ((ITERS + 1, ROWS, COLS), (ROWS, COLS), (ROWS, COLS), (nx * ny, COLS))
        ),
        scratch_shapes=[
            pltpu.VMEM((DEEP_SIZE, COLS), f32),
            pltpu.VMEM((DEEP_SIZE, COLS), f32),
            pltpu.VMEM((DEEP_SIZE, COLS), f32),
            pltpu.VMEM((4, LEVELS, ROWS, COLS), f32),
            pltpu.VMEM((4, LEVELS, ROWS, COLS), f32),
            pltpu.VMEM((LEVELS, ROWS, COLS), f32),
            pltpu.VMEM((LEVELS, ROWS, COLS), f32),
            pltpu.VMEM((4, ROWS, COLS), f32),
        ],
        name="krylov",
    )(fold_map, tracer, *rest)

    moments = lax.all_to_all(partial, BOTH, 0, 0)

    batch = pl.BlockSpec((GROUP, LEVELS, ROWS, COLS), lambda i: (i, 0, 0, 0))
    edge = pl.BlockSpec((TRACERS * LEVELS, COLS), lambda i: (0, 0))
    tiles = pl.BlockSpec((COL_DEEP, COLS), lambda i: (0, 0))
    mixed = kernel(
        tracers_kernel,
        grid=(TRACERS // GROUP,),
        out_shape=shape(TRACERS, LEVELS, ROWS, COLS),
        in_specs=[smem, batch] + [all_of(array) for array in (*fields, level_count)] + [tiles, tiles, edge, edge, edge],
        out_specs=batch,
        scratch_shapes=[
            pltpu.VMEM((TRACERS * LEVELS, COLS), f32),
            pltpu.VMEM((TRACERS * LEVELS, COLS), f32),
            pltpu.VMEM((8, LEVELS, ROWS, COLS), f32),
        ],
        name="tracers",
    )(fold_map, tracer, *fields, level_count, from_east, from_west, near, far, extra)

    pressure, residual, good = kernel(
        combine_kernel,
        out_shape=(shape(ROWS, COLS), shape(ROWS, COLS), jax.ShapeDtypeStruct((1,), jnp.int32)),
        in_specs=[whole()] * 3,
        out_specs=(whole(), whole(), smem),
        name="combine",
    )(moments, vectors, diagonal)

    pressure, residual = lax.cond(
        good[0] == 1,
        lambda pressure, residual, rhs, count, surface, fold: (pressure, residual),
        lambda pressure, residual, rhs, count, surface, fold: direct_gradients(rhs, count, fold, surface),
        pressure,
        residual,
        rhs,
        level_count,
        surface_term,
        fold_map,
    )
    return mixed, pressure, residual


def solution(mesh):
    in_specs = (
        P(None, None, "gy", "gx"),
        P(None, "gy", "gx"),
        P(None, "gy", "gx"),
        P(None, "gy", "gx"),
        P(None, "gy", "gx"),
        P("gy", "gx"),
        P(),
        P("gy", "gx"),
    )
    out_specs = (P(None, None, "gy", "gx"), P("gy", "gx"), P("gy", "gx"))
    body = functools.partial(shards, (mesh.shape["gx"], mesh.shape["gy"]))
    return jax.shard_map(body, mesh=mesh, in_specs=in_specs, out_specs=out_specs, check_vma=False)
```

time: 734 us -> 66.9 us (0.09)
  blocking collectives: 524 us -> 0 us
  waiting for transfers between devices: 60.7 us -> 16.6 us
  local copies, waits for them, and re-layouts: 40.6 us -> 6 us
  other arithmetic: 28.9 us -> 0 us
  between operations: 24.7 us -> 2.14 us
  starting transfers between devices: 53.3 us -> 31.5 us
  Pallas kernels: 0 us -> 10.2 us
    psum x7 -> x0, blocking collectives: 451 us -> none  [the longest x4 255 us: residual_energy(): return lax.psum(jnp.sum(resid * scaled_now), ('gx', 'gy'))]
    all_gather x5 -> x0, blocking collectives: 72.8 us -> none  [extend(): whole_row = lax.all_gather(top_row, 'gx', axis=2, tiled=True)]
    ppermute x24 -> x5, starting transfers between devices: 53.3 us -> 13.8 us  [the longest x1 7.11 us: shards(): lax.ppermute(to_west, BOTH, [(device(x + 1, y), device(x, y)) for x in ra...]
    ppermute x24 -> x5, waiting for transfers between devices: 41.7 us -> 11.3 us  [the longest x1 5.4 us: exchange(): lax.ppermute(rows, BOTH, inner + across(even))]
    all_gather x1 -> x0, waiting for transfers between devices: 18.9 us -> none  [extend(): whole_row = lax.all_gather(top_row, 'gx', axis=2, tiled=True)]
    all_to_all x0 -> x1, starting transfers between devices: none -> 17.8 us  [shards(): moments = lax.all_to_all(partial, BOTH, 0, 0)]
    gather x7 -> x0, local copies, waits for them, and re-layouts: 16.5 us -> none  [extend(): folded = jnp.take(whole_row, partner, axis=2)]
    all_gather x1 -> x0, local copies, waits for them, and re-layouts: 12.5 us -> none  [extend(): whole_row = lax.all_gather(top_row, 'gx', axis=2, tiled=True)]
  transfers between devices with their start and end apart: 25 -> 6, of which waited for: 21 -> 4; matrix products, arithmetic and copies ran while one was open for 6% -> 1% of each run, Pallas kernels for 0% -> 7%
where the time goes in v1:
time: 66.9 us; the launch traced here: 66.8 us
  starting transfers between devices  31.5 us (47%)
  waiting for transfers between devices  16.6 us (25%)
  Pallas kernels  10.2 us (15%)
  local copies, waits for them, and re-layouts  6 us (9%)
  between operations  2.14 us (3%)
    all_to_all x1, starting transfers between devices, shards(): moments = lax.all_to_all(partial, BOTH, 0, 0)  17.8 us
    ppermute x1, starting transfers between devices, shards(): lax.ppermute(to_west, BOTH, [(device(x + 1, y), device(x, y)) for x in ra...  7.11 us
    unnamed x28, local copies, waits for them, and re-layouts  5.49 us
    ppermute x1, waiting for transfers between devices, exchange(): lax.ppermute(rows, BOTH, inner + across(even))  5.4 us
    all_to_all x1, waiting for transfers between devices, shards(): moments = lax.all_to_all(partial, BOTH, 0, 0)  5.35 us
    ppermute x1, waiting for transfers between devices, shards(): lax.ppermute(to_east, BOTH, [(device(x - 1, y), device(x, y)) for x in ra...  5.07 us
    pallas_call x1, Pallas kernels, shards(): kernel(tracers_kernel, grid=(TRACERS // GROUP,), out_shape=shape(TRACERS,...  4.25 us
    pallas_call x1, Pallas kernels, shards(): kernel(krylov_kernel, grid=(1,), out_shape=(shape(ITERS + 1, ROWS, COLS),...  3.29 us
  transfers between devices with their start and end apart: 6, of which 4 were waited for; matrix products, arithmetic and copies ran while one was open for 1% of the time, Pallas kernels for 7%

profile of v1, /device:TPU:1, one launch (start us, length us, event | category | flops | bytes accessed | tf_op | source)
XLA Modules:
  0.0 66.8 jit_solution(16363587865183910766)
XLA Ops:
  0.6 0.0 copy-start
  0.6 1.3 %copy-done = f32[16,20,8,128]{3,2,1,0:T(8,128)S(1)} copy-done((f32[16,20,8,128]{3,2,1,0:T(8,128)S(1)}, f32[16,20,8,128]{3,2,1,0:T(8,128)}, u32[]{:S(2)}) %copy-start) | copy-done | bytes 1310744
  2.0 0.9 %copy-done.2 = f32[20,8,128]{2,1,0:T(8,128)S(1)} copy-done((f32[20,8,128]{2,1,0:T(8,128)S(1)}, f32[20,8,128]{2,1,0:T(8,128)}, u32[]{:S(2)}) %copy-start.2) | copy-done | bytes 81944
  2.8 0.9 %copy-done.4 = f32[20,8,128]{2,1,0:T(8,128)S(1)} copy-done((f32[20,8,128]{2,1,0:T(8,128)S(1)}, f32[20,8,128]{2,1,0:T(8,128)}, u32[]{:S(2)}) %copy-start.4) | copy-done | bytes 81944
  3.7 0.9 %copy-done.6 = f32[20,8,128]{2,1,0:T(8,128)S(1)} copy-done((f32[20,8,128]{2,1,0:T(8,128)S(1)}, f32[20,8,128]{2,1,0:T(8,128)}, u32[]{:S(2)}) %copy-start.6) | copy-done | bytes 81944
  4.6 0.9 %copy-done.8 = f32[20,8,128]{2,1,0:T(8,128)S(1)} copy-done((f32[20,8,128]{2,1,0:T(8,128)S(1)}, f32[20,8,128]{2,1,0:T(8,128)}, u32[]{:S(2)}) %copy-start.8) | copy-done | bytes 81944
  5.5 1.7 %pack_columns.1 = (f32[72,128]{1,0:T(8,128)S(1)}, f32[72,128]{1,0:T(8,128)S(1)}) custom-call(f32[16,20,8,128]{3,2,1,0:T(8,128)S(1)} %copy-done, f32[20,8,128]{2,1,0:T(8,128)S(1)} %copy-done.2, f32[20,8,128]{2,1,0:T(8,128)S(1)} %copy-done.4, f32[20,8,128]{2,1,0:T(8,128)S(1)} %copy-done.6, f32[20,8,128]{2,1,0:T(8,128)S(1)} %copy-done.8, s32[8,128]{1,0:T(8,128)} %count.7, ...), custom_call_target="tpu_custom_call" | custom-call | tf_op jit(solution)/shard_map/pack_columns/pallas_call | solution.py:698
  7.2 7.1 %collective-permute-start.40 = (f32[72,128]{1,0:T(8,128)S(1)}, f32[72,128]{1,0:T(8,128)S(1)}, u32[]{:S(2)}, u32[]{:S(2)}) collective-permute-start(f32[72,128]{1,0:T(8,128)S(1)} %get-tuple-element.254), channel_id=1, source_target_pairs={{8,0},{9,1},{10,2},{11,3},{12,4},{13,5},{14,6},{15,7},{16,8},{17,9... | collective-permute-start | bytes 110600 | tf_op jit(solution)/shard_map/ppermute | solution.py:705
  14.4 0.2 pack_rows.1
  14.6 0.8 %collective-permute-done.40.east.from_east = f32[72,128]{1,0:T(8,128)S(1)} collective-permute-done((f32[72,128]{1,0:T(8,128)S(1)}, f32[72,128]{1,0:T(8,128)S(1)}, u32[]{:S(2)}, u32[]{:S(2)}) %collective-permute-start.40) | collective-permute-done | bytes 36896 | tf_op jit(solution)/shard_map/ppermute | solution.py:705
  15.4 5.1 %collective-permute-done.41.west.from_west = f32[72,128]{1,0:T(8,128)S(1)} collective-permute-done((f32[72,128]{1,0:T(8,128)S(1)}, f32[72,128]{1,0:T(8,128)S(1)}, u32[]{:S(2)}, u32[]{:S(2)}) %collective-permute-start.41) | collective-permute-done | bytes 36896 | tf_op jit(solution)/shard_map/ppermute | solution.py:706
  20.5 2.2 %collective-permute-start.42 = (f32[896,128]{1,0:T(8,128)S(1)}, f32[896,128]{1,0:T(8,128)S(1)}, u32[]{:S(2)}, u32[]{:S(2)}) collective-permute-start(f32[896,128]{1,0:T(8,128)S(1)} %get-tuple-element.258), channel_id=1, source_target_pairs={{1,0},{0,1},{3,2},{2,3},{5,4},{4,5},{7,6},{6,7},{9,8},{8,9},{11,10... | collective-permute-start | bytes 1376264 | tf_op jit(solution)/shard_map/ppermute | solution.py:730
  22.7 0.5 slice.136
  23.9 9.9 %conditional.2 = (f32[896,128]{1,0:T(8,128)}, f32[896,128]{1,0:T(8,128)}) conditional(s32[]{:T(128)} %clamp.3, f32[896,128]{1,0:T(8,128)S(1)} %get-tuple-element.259, f32[896,128]{1,0:T(8,128)S(1)} %get-tuple-element.259, f32[896,128]{1,0:T(8,128)S(1)} %get-tuple-element.259, ...), branch_computations={%region_0.1_spmd, %region_1.2_spmd, %region_2.3_spmd, %region_3.4_... | conditional | bytes 3670112 | solution.py:744
  23.9 3.0 %collective-permute-start = (f32[896,128]{1,0:T(8,128)S(1)}, f32[896,128]{1,0:T(8,128)}, u32[]{:S(2)}, u32[]{:S(2)}) collective-permute-start(f32[896,128]{1,0:T(8,128)S(1)} %param), channel_id=1, source_target_pairs={{2,1},{1,2},{4,3},{3,4},{6,5},{5,6},{10,9},{9,10},{12,11},{11,12},... | collective-permute-start | bytes 1376264 | tf_op jit(solution)/shard_map/cond/branch_0_fun/ppermute | solution.py:741
  26.9 1.5 %collective-permute-start.1 = (f32[896,128]{1,0:T(8,128)S(1)}, f32[896,128]{1,0:T(8,128)}, u32[]{:S(2)}, u32[]{:S(2)}) collective-permute-start(f32[896,128]{1,0:T(8,128)S(1)} %param), channel_id=1, source_target_pairs={{127,7},{119,15},{111,23},{103,31},{95,39},{87,47},{79,55},{71,63}... | collective-permute-start | bytes 1376264 | tf_op jit(solution)/shard_map/cond/branch_0_fun/ppermute | solution.py:741
  28.4 5.4 %collective-permute-done = f32[896,128]{1,0:T(8,128)} collective-permute-done((f32[896,128]{1,0:T(8,128)S(1)}, f32[896,128]{1,0:T(8,128)}, u32[]{:S(2)}, u32[]{:S(2)}) %collective-permute-start) | collective-permute-done | bytes 458784 | tf_op jit(solution)/shard_map/cond/branch_0_fun/ppermute | solution.py:741
  33.9 3.3 %krylov.1 = (f32[5,8,128]{2,1,0:T(8,128)S(1)}, f32[8,128]{1,0:T(8,128)S(1)}, f32[8,128]{1,0:T(8,128)S(1)}, f32[128,128]{1,0:T(8,128)}) custom-call(s32[2048]{0:T(1024)S(1)} %copy-done.10, f32[16,20,8,128]{3,2,1,0:T(8,128)S(1)} %copy-done.1, f32[20,8,128]{2,1,0:T(8,128)S(1)} %copy-done.3, f32[20,8,128]{2,1,0:T(8,128)S(1)} %copy-done.5, ...), custom_call_target="tpu_custom_call" | custom-call | tf_op jit(solution)/shard_map/krylov/pallas_call | solution.py:753
  37.2 17.8 %all-to-all-start = ((f32[128,1,128]{2,1,0:T(1,128)}), f32[128,1,128]{2,1,0:T(1,128)S(1)}, u32[]{:S(2)}, u32[]{:S(2)}) async-start(f32[128,1,128]{2,1,0:T(1,128)} %bitcast.6), calls=%async_computation | async-start | bytes 131072 | tf_op jit(solution)/shard_map/all_to_all | solution.py:775
  54.9 4.3 %tracers.1 = f32[16,20,8,128]{3,2,1,0:T(8,128)} custom-call(s32[2048]{0:T(1024)S(1)} %copy-done.10, f32[16,20,8,128]{3,2,1,0:T(8,128)S(1)} %copy-done.1, f32[20,8,128]{2,1,0:T(8,128)S(1)} %copy-done.3, f32[20,8,128]{2,1,0:T(8,128)S(1)} %copy-done.5, f32[20,8,128]{2,1,0:T(8,128)S(1)} %copy-done.7, f32[20,8,128]{2,1,0:T(8,128)S(1)} %copy-done.9, ...), custom_call_target="tpu_custom_call" | custom-call | tf_op jit(solution)/shard_map/tracers/pallas_call | solution.py:780
  59.2 5.4 %all-to-all-done = f32[128,1,128]{2,1,0:T(1,128)S(1)} async-done(((f32[128,1,128]{2,1,0:T(1,128)}), f32[128,1,128]{2,1,0:T(1,128)S(1)}, u32[]{:S(2)}, u32[]{:S(2)}) %all-to-all-start) | async-done | bytes 65568 | tf_op jit(solution)/shard_map/all_to_all | solution.py:775
  64.5 0.8 %combine.1 = (f32[8,128]{1,0:T(8,128)}, f32[8,128]{1,0:T(8,128)S(1)}, s32[1]{0:T(128)}) custom-call(f32[128,128]{1,0:T(8,128)S(1)} %bitcast.20, f32[5,8,128]{2,1,0:T(8,128)S(1)} %get-tuple-element.263.vectors, f32[8,128]{1,0:T(8,128)S(1)} %get-tuple-element.264.diagonal), custom_call_target="tpu_custom_call" | custom-call | tf_op jit(solution)/shard_map/combine/pallas_call | solution.py:794
  66.0 0.2 conditional.3
  66.2 0.6 copy-done.12
  (26 shorter events, 0.1 us)
Async XLA Ops:
  0.6 1.3 %copy-start = (f32[16,20,8,128]{3,2,1,0:T(8,128)S(1)}, f32[16,20,8,128]{3,2,1,0:T(8,128)}, u32[]{:S(2)}) copy-start(f32[16,20,8,128]{3,2,1,0:T(8,128)} %tracer.5) | copy-start | bytes 3932164
  1.9 0.9 %copy-start.2 = (f32[20,8,128]{2,1,0:T(8,128)S(1)}, f32[20,8,128]{2,1,0:T(8,128)}, u32[]{:S(2)}) copy-start(f32[20,8,128]{2,1,0:T(8,128)} %east_vel.7) | copy-start | bytes 245764
  2.8 0.9 %copy-start.4 = (f32[20,8,128]{2,1,0:T(8,128)S(1)}, f32[20,8,128]{2,1,0:T(8,128)}, u32[]{:S(2)}) copy-start(f32[20,8,128]{2,1,0:T(8,128)} %north_vel.7) | copy-start | bytes 245764
  3.7 0.9 %copy-start.6 = (f32[20,8,128]{2,1,0:T(8,128)S(1)}, f32[20,8,128]{2,1,0:T(8,128)}, u32[]{:S(2)}) copy-start(f32[20,8,128]{2,1,0:T(8,128)} %diffusion.7) | copy-start | bytes 245764
  4.6 0.9 %copy-start.8 = (f32[20,8,128]{2,1,0:T(8,128)S(1)}, f32[20,8,128]{2,1,0:T(8,128)}, u32[]{:S(2)}) copy-start(f32[20,8,128]{2,1,0:T(8,128)} %mixing.7) | copy-start | bytes 245764
  5.5 8.8 %copy-start.11 = (s32[8,128]{1,0:T(8,128)S(1)}, s32[8,128]{1,0:T(8,128)}, u32[]{:S(2)}) copy-start(s32[8,128]{1,0:T(8,128)} %count.7) | copy-start | bytes 12292
  5.5 8.8 %copy-start.13 = (f32[8,128]{1,0:T(8,128)S(1)}, f32[8,128]{1,0:T(8,128)}, u32[]{:S(2)}) copy-start(f32[8,128]{1,0:T(8,128)} %surface.5) | copy-start | bytes 12292
  7.2 8.2 %collective-permute-start.40 = (f32[72,128]{1,0:T(8,128)S(1)}, f32[72,128]{1,0:T(8,128)S(1)}, u32[]{:S(2)}, u32[]{:S(2)}) collective-permute-start(f32[72,128]{1,0:T(8,128)S(1)} %get-tuple-element.254), channel_id=1, source_target_pairs={{8,0},{9,1},{10,2},{11,3},{12,4},{13,5},{14,6},{15,7},{16,8},{17,9... | collective-permute-start | bytes 110600 | tf_op jit(solution)/shard_map/ppermute | solution.py:705
  14.3 6.1 %collective-permute-start.41 = (f32[72,128]{1,0:T(8,128)S(1)}, f32[72,128]{1,0:T(8,128)S(1)}, u32[]{:S(2)}, u32[]{:S(2)}) collective-permute-start(f32[72,128]{1,0:T(8,128)S(1)} %get-tuple-element.255), channel_id=1, source_target_pairs={{120,0},{121,1},{122,2},{123,3},{124,4},{125,5},{126,6},{127,7},{0... | collective-permute-start | bytes 110600 | tf_op jit(solution)/shard_map/ppermute | solution.py:706
  14.4 8.3 %copy-start.10 = (s32[2048]{0:T(1024)S(1)}, s32[2048]{0:T(1024)}, u32[]{:S(2)}) copy-start(s32[2048]{0:T(1024)} %fold_map.3) | copy-start | bytes 24580
  14.4 19.5 %copy-start.1 = (f32[16,20,8,128]{3,2,1,0:T(8,128)S(1)}, f32[16,20,8,128]{3,2,1,0:T(8,128)}, u32[]{:S(2)}) copy-start(f32[16,20,8,128]{3,2,1,0:T(8,128)} %tracer.5) | copy-start | bytes 3932164
  14.4 19.4 %copy-start.3 = (f32[20,8,128]{2,1,0:T(8,128)S(1)}, f32[20,8,128]{2,1,0:T(8,128)}, u32[]{:S(2)}) copy-start(f32[20,8,128]{2,1,0:T(8,128)} %east_vel.7) | copy-start | bytes 245764
  14.4 19.4 %copy-start.5 = (f32[20,8,128]{2,1,0:T(8,128)S(1)}, f32[20,8,128]{2,1,0:T(8,128)}, u32[]{:S(2)}) copy-start(f32[20,8,128]{2,1,0:T(8,128)} %north_vel.7) | copy-start | bytes 245764
  14.4 19.4 %copy-start.7 = (f32[20,8,128]{2,1,0:T(8,128)S(1)}, f32[20,8,128]{2,1,0:T(8,128)}, u32[]{:S(2)}) copy-start(f32[20,8,128]{2,1,0:T(8,128)} %diffusion.7) | copy-start | bytes 245764
  14.4 19.4 %copy-start.9 = (f32[20,8,128]{2,1,0:T(8,128)S(1)}, f32[20,8,128]{2,1,0:T(8,128)}, u32[]{:S(2)}) copy-start(f32[20,8,128]{2,1,0:T(8,128)} %mixing.7) | copy-start | bytes 245764
  20.5 13.3 %collective-permute-start.42 = (f32[896,128]{1,0:T(8,128)S(1)}, f32[896,128]{1,0:T(8,128)S(1)}, u32[]{:S(2)}, u32[]{:S(2)}) collective-permute-start(f32[896,128]{1,0:T(8,128)S(1)} %get-tuple-element.258), channel_id=1, source_target_pairs={{1,0},{0,1},{3,2},{2,3},{5,4},{4,5},{7,6},{6,7},{9,8},{8,9},{11,10... | collective-permute-start | bytes 1376264 | tf_op jit(solution)/shard_map/ppermute | solution.py:730
  23.9 9.9 %collective-permute-start = (f32[896,128]{1,0:T(8,128)S(1)}, f32[896,128]{1,0:T(8,128)}, u32[]{:S(2)}, u32[]{:S(2)}) collective-permute-start(f32[896,128]{1,0:T(8,128)S(1)} %param), channel_id=1, source_target_pairs={{2,1},{1,2},{4,3},{3,4},{6,5},{5,6},{10,9},{9,10},{12,11},{11,12},... | collective-permute-start | bytes 1376264 | tf_op jit(solution)/shard_map/cond/branch_0_fun/ppermute | solution.py:741
  26.9 6.9 %collective-permute-start.1 = (f32[896,128]{1,0:T(8,128)S(1)}, f32[896,128]{1,0:T(8,128)}, u32[]{:S(2)}, u32[]{:S(2)}) collective-permute-start(f32[896,128]{1,0:T(8,128)S(1)} %param), channel_id=1, source_target_pairs={{127,7},{119,15},{111,23},{103,31},{95,39},{87,47},{79,55},{71,63}... | collective-permute-start | bytes 1376264 | tf_op jit(solution)/shard_map/cond/branch_0_fun/ppermute | solution.py:741
  37.2 27.4 %all-to-all-start = ((f32[128,1,128]{2,1,0:T(1,128)}), f32[128,1,128]{2,1,0:T(1,128)S(1)}, u32[]{:S(2)}, u32[]{:S(2)}) async-start(f32[128,1,128]{2,1,0:T(1,128)} %bitcast.6), calls=%async_computation | async-start | bytes 131072 | tf_op jit(solution)/shard_map/all_to_all | solution.py:775
  66.2 0.6 copy-start.12

commit v2 on v0

v2 whole, which is shorter than its diff:
```python
import functools

import jax
import jax.numpy as jnp
from jax import lax
from jax.experimental import pallas as pl
from jax.experimental.pallas import tpu as pltpu
from jax.sharding import PartitionSpec as P

ITERS = 4
TRACERS, LEVELS, ROWS, COLS = 16, 20, 8, 128
GROUP = 4
GROUPS = TRACERS // GROUP
EDGE = TRACERS * LEVELS
BOTH = ("gx", "gy")
VMEM_LIMIT = 40 * 1024 * 1024


def params():
    return pltpu.CompilerParams(vmem_limit_bytes=VMEM_LIMIT)


def whole():
    return pl.BlockSpec(memory_space=pltpu.VMEM)


def lanes():
    return lax.broadcasted_iota(jnp.int32, (ROWS, COLS), 1)


def sublanes():
    return lax.broadcasted_iota(jnp.int32, (ROWS, COLS), 0)


def roll(tile, shift, axis):
    size = tile.shape[axis]
    shift = shift % size
    return tile if shift == 0 else pltpu.roll(tile, shift, axis)


def east_of(tile, beyond, lane):
    return roll(jnp.where(lane == 0, beyond, tile), -1, 1)


def west_of(tile, beyond, lane):
    return roll(jnp.where(lane == COLS - 1, beyond, tile), 1, 1)


def north_of(tile, beyond, sub):
    return roll(jnp.where(sub == 0, beyond, tile), -1, 0)


def south_of(tile, beyond, sub):
    return roll(jnp.where(sub == ROWS - 1, beyond, tile), 1, 0)


def thickness(level):
    return 0.5 + 1.5 * level / (LEVELS - 1)


def pack_kernel(
    tracer, count, surface,
    to_west, to_east, near, far, shared,
    cells, levels_ref, surface_ref, ready,
):
    lane = lanes()
    size = GROUP * LEVELS * ROWS
    small = [
        pltpu.make_async_copy(count, levels_ref, ready.at[GROUPS]),
        pltpu.make_async_copy(surface, surface_ref, ready.at[GROUPS + 1]),
    ]
    large = [
        pltpu.make_async_copy(tracer.at[pl.ds(g * size, size)], cells.at[pl.ds(g * size, size)], ready.at[g])
        for g in range(GROUPS)
    ]
    for copy in small + large:
        copy.start()
    even = lax.axis_index("gy") % 2 == 0
    for copy in small:
        copy.wait()
    levels = levels_ref[...]
    depth = jnp.zeros((ROWS, COLS), jnp.float32)
    for k in range(LEVELS):
        depth = depth + jnp.where(k < levels, thickness(k), 0.0)
    shared[:, :ROWS, :] = jnp.broadcast_to((depth / LEVELS)[None], (shared.shape[0], ROWS, COLS))
    shared[:, ROWS:, :] = jnp.broadcast_to(surface_ref[...][None], (shared.shape[0], ROWS, COLS))

    per = 2 * LEVELS
    level_row = lax.broadcasted_iota(jnp.int32, (per, COLS), 0)
    level_row = jnp.where(level_row >= LEVELS, level_row - LEVELS, level_row)
    wet_south = level_row < jnp.broadcast_to(levels[:1, :], (per, COLS))
    wet_north = level_row < jnp.broadcast_to(levels[ROWS - 1 :, :], (per, COLS))
    for g in range(GROUPS):
        large[g].wait()
        west = jnp.zeros((ROWS, COLS), jnp.float32)
        east = jnp.zeros((ROWS, COLS), jnp.float32)
        for t in range(GROUP):
            for k in range(LEVELS):
                row, first = ((g * GROUP + t) * LEVELS + k) * ROWS, t * LEVELS + k
                tile = jnp.where(k < levels, cells[row : row + ROWS, :], 0.0)
                west = jnp.where(lane == first, roll(tile, first, 1), west)
                east = jnp.where(lane == first, roll(tile, first + 1, 1), east)
        to_west[g * ROWS : (g + 1) * ROWS, :] = west
        to_east[g * ROWS : (g + 1) * ROWS, :] = east
        for half in range(GROUP * LEVELS // per):
            at = g * GROUP * LEVELS + half * per
            south = jnp.where(wet_south, cells[pl.ds(at * ROWS, per, stride=ROWS), :], 0.0)
            north = jnp.where(wet_north, cells[pl.ds(at * ROWS + ROWS - 1, per, stride=ROWS), :], 0.0)
            near[at : at + per, :] = jnp.where(even, north, south)
            far[at : at + per, :] = jnp.where(even, south, north)


def pole_of(fold_map):
    return (fold_map[0] + 1) & (COLS * lax.axis_size("gx") - 1)


def halo_rows(fold_map, near, far, extra, north_rows, south_rows):
    here = lax.axis_index("gy")
    top = lax.axis_size("gy") - 1

    @pl.when(here % 2 == 0)
    def _():
        north_rows[...] = near[...]
        south_rows[...] = far[...]

    @pl.when(here % 2 == 1)
    def _():
        south_rows[...] = near[...]

    @pl.when((here % 2 == 1) & (here != top))
    def _():
        north_rows[...] = far[...]

    @pl.when(here == top)
    def _():
        lane = lanes()
        pole = pole_of(fold_map)
        offset = pole & (COLS - 1)
        index = (offset - 1 - lane) & (COLS - 1)
        from_far = (lane >= offset) == ((pole & COLS) != 0)
        for row in range(0, north_rows.shape[0], ROWS):
            a = jnp.take_along_axis(far[row : row + ROWS, :], index, axis=1)
            b = jnp.take_along_axis(extra[row : row + ROWS, :], index, axis=1)
            north_rows[row : row + ROWS, :] = jnp.where(from_far, a, b)


def right_side_kernel(
    fold_map, tracer, east_vel, north_vel, diffusion, mixing, count, from_east, from_west, near, far, extra,
    rhs,
    north_rows, south_rows,
):
    lane, sub = lanes(), sublanes()
    levels = count[...]
    halo_rows(fold_map, near, far, extra, north_rows, south_rows)

    def gap(rows, k):
        return rows[k : k + 1, :] - rows[LEVELS + k : LEVELS + k + 1, :]

    columns_east = from_east[...] - roll(from_east[...], -LEVELS, 1)
    columns_west = from_west[...] - roll(from_west[...], -LEVELS, 1)
    zero = jnp.zeros((ROWS, COLS), jnp.float32)
    c_prev, r_prev, a_prev = zero, zero, zero
    c_list, r_list = [], []
    for k in range(LEVELS):
        wet = k < levels
        cell = jnp.where(wet, tracer[0, k] - tracer[1, k], 0.0)
        east = east_of(cell, roll(columns_east, -k, 1), lane)
        west = west_of(cell, roll(columns_west, COLS - 1 - k, 1), lane)
        north = north_of(cell, gap(north_rows, k), sub)
        south = south_of(cell, gap(south_rows, k), sub)
        change = (
            -0.5 * east_vel[k] * (east - west)
            - 0.5 * north_vel[k] * (north - south)
            + diffusion[k] * (east + west + north + south - 4.0 * cell)
        )
        explicit = cell + jnp.where(wet, change, 0.0)
        a = jnp.where(k + 1 < levels, mixing[k], 0.0)
        inverse = 1.0 / (1.0 + a_prev + a + a_prev * c_prev)
        c_prev = -a * inverse
        r_prev = (explicit + a_prev * r_prev) * inverse
        a_prev = a
        c_list.append(c_prev)
        r_list.append(r_prev)
    total, x_next = zero, zero
    for k in range(LEVELS - 1, -1, -1):
        x_next = r_list[k] - c_list[k] * x_next
        total = total + thickness(k) * x_next
    value = jnp.where(levels > 0, 0.25 * total, 0.0)
    rhs[...] = jnp.broadcast_to(value[None], rhs.shape)


def gradients_kernel(
    fold_map, rhs, shared,
    pressure, residual,
    to_e, to_w, from_n, from_ne, from_nw, from_s, from_se, from_sw, diagonal, inverse, scaled, field, image, ghost,
):
    nx, ny = lax.axis_size("gx"), lax.axis_size("gy")
    lane, sub = lanes(), sublanes()
    zero = jnp.zeros((ROWS, COLS), jnp.float32)
    pole = pole_of(fold_map)

    def tile(ref, x, y):
        return ref[pl.ds(pl.multiple_of((x * ny + y) * ROWS, ROWS), ROWS), :]

    def put(ref, x, y, value):
        ref[pl.ds(pl.multiple_of((x * ny + y) * ROWS, ROWS), ROWS), :] = value

    def strip(ref, x):
        return [tile(ref, x, y) for y in range(ny)]

    def beside(ref, x):
        own = strip(ref, x)
        after, before = strip(ref, (x + 1) & (nx - 1)), strip(ref, (x - 1) & (nx - 1))
        east = [east_of(own[y], after[y], lane) for y in range(ny)]
        west = [west_of(own[y], before[y], lane) for y in range(ny)]
        return own, east, west

    def moved_south(tiles, last):
        return [north_of(tiles[y], tiles[y + 1] if y + 1 < ny else last, sub) for y in range(ny)]

    def moved_north(tiles):
        return [south_of(tiles[y], tiles[y - 1] if y else zero, sub) for y in range(ny)]

    def over_fold(ref, shift):
        turn = (pole - 1 - shift) & (nx * COLS - 1)
        offset, block = (turn + 1) & (COLS - 1), ((turn + 1) >> (COLS.bit_length() - 1)) & (nx - 1)
        rows = ref[pl.ds(ny * ROWS - 1, nx, stride=ny * ROWS), :]
        index = (offset - 1 - lane) & (COLS - 1)
        halves = [jnp.take_along_axis(rows[h : h + ROWS, :], index, axis=1) for h in range(0, nx, ROWS)]
        out = []
        for h in range(0, nx, ROWS):
            ends = []
            for turned in (block - 1, block):
                source = (turned - h - sub) & (nx - 1)
                value = jnp.take_along_axis(halves[0], source & (ROWS - 1), axis=0)
                for at in range(1, nx // ROWS):
                    other = jnp.take_along_axis(halves[at], source & (ROWS - 1), axis=0)
                    value = jnp.where(source >= at * ROWS, other, value)
                ends.append(value)
            out.append(jnp.where(lane >= offset, ends[0], ends[1]))
        return out

    def last_rows(ref):
        rows = ref[pl.ds(ny * ROWS - 1, nx, stride=ny * ROWS), :]
        return [rows[h : h + ROWS, :] for h in range(0, nx, ROWS)]

    def put_ghost(values):
        for at, value in enumerate(values):
            ghost[at * ROWS : (at + 1) * ROWS, :] = value

    def total(value):
        return jnp.broadcast_to(jnp.sum(value, keepdims=True), (ROWS, COLS))

    def spread(x, carry):
        for y in range(ny):
            put(field, x, y, shared[x * ny + y, :ROWS, :])
        return carry

    lax.fori_loop(0, nx, spread, 0)
    edge, beyond = last_rows(field), over_fold(field, 0)
    beyond_e, beyond_w = over_fold(field, 1), over_fold(field, -1)
    fold_n = [jnp.minimum(a, b) for a, b in zip(edge, beyond)]
    fold_ne = [0.5 * jnp.minimum(a, b) for a, b in zip(edge, beyond_e)]
    fold_nw = [0.5 * jnp.minimum(a, b) for a, b in zip(edge, beyond_w)]
    put_ghost([a + b + c for a, b, c in zip(fold_n, fold_ne, fold_nw)])

    def couple(x, energy):
        own, east, west = beside(field, x)
        above = moved_south(own, zero)
        below = moved_north(own)
        side, ahead, behind = [], [], []
        for y in range(ny):
            e, w = jnp.minimum(own[y], east[y]), jnp.minimum(own[y], west[y])
            n, ne, nw = (
                jnp.minimum(below[y], own[y]),
                0.5 * jnp.minimum(below[y], east[y]),
                0.5 * jnp.minimum(below[y], west[y]),
            )
            s, se, sw = (
                jnp.minimum(above[y], own[y]),
                0.5 * jnp.minimum(above[y], east[y]),
                0.5 * jnp.minimum(above[y], west[y]),
            )
            for ref, value in zip(
                (to_e, to_w, from_n, from_ne, from_nw, from_s, from_se, from_sw), (e, w, n, ne, nw, s, se, sw)
            ):
                put(ref, x, y, value)
            side.append(e + w)
            ahead.append(n + ne + nw)
            behind.append(s + se + sw)
        ahead = moved_south(ahead, ghost[pl.ds(x, 1), :])
        behind = moved_north(behind)
        for y in range(ny):
            term = shared[x * ny + y, ROWS:, :] + (side[y] + ahead[y] + behind[y])
            diag = jnp.where(own[y] > 0.0, term, 1.0)
            inv = 1.0 / diag
            resid = tile(rhs, x, y)
            first = resid * inv
            put(diagonal, x, y, diag)
            put(inverse, x, y, inv)
            put(scaled, x, y, first)
            energy = energy + resid * first
        return energy

    energy = total(lax.fori_loop(0, nx, couple, zero))

    def start(x, carry):
        for y in range(ny):
            put(field, x, y, tile(scaled, x, y))
            put(scaled, x, y, tile(rhs, x, y))
        return carry

    lax.fori_loop(0, nx, start, 0)

    my_x, my_y = lax.axis_index("gx"), lax.axis_index("gy")
    mine = zero
    for step in range(ITERS):
        beyond = zip(fold_n, over_fold(field, 0), fold_ne, over_fold(field, 1), fold_nw, over_fold(field, -1))
        put_ghost([a * p + b * q + c * r for a, p, b, q, c, r in beyond])

        def apply(x, product):
            own, east, west = beside(field, x)
            ahead, behind = [], []
            for y in range(ny):
                ahead.append(
                    tile(from_n, x, y) * own[y] + tile(from_ne, x, y) * east[y] + tile(from_nw, x, y) * west[y]
                )
                behind.append(
                    tile(from_s, x, y) * own[y] + tile(from_se, x, y) * east[y] + tile(from_sw, x, y) * west[y]
                )
            ahead = moved_south(ahead, ghost[pl.ds(x, 1), :])
            behind = moved_north(behind)
            for y in range(ny):
                side = tile(to_e, x, y) * east[y] + tile(to_w, x, y) * west[y]
                value = tile(diagonal, x, y) * own[y] - (side + ahead[y] + behind[y])
                put(image, x, y, value)
                product = product + own[y] * value
            return product

        step_size = energy / total(lax.fori_loop(0, nx, apply, zero))
        mine = mine + step_size * tile(field, my_x, my_y)
        if step + 1 == ITERS:
            break

        def reduce(x, sums):
            for y in range(ny):
                resid = tile(scaled, x, y) - step_size * tile(image, x, y)
                put(scaled, x, y, resid)
                sums = sums + resid * (resid * tile(inverse, x, y))
            return sums

        energy_new = total(lax.fori_loop(0, nx, reduce, zero))
        ratio = energy_new / energy
        energy = energy_new

        def turn(x, carry):
            for y in range(ny):
                put(field, x, y, tile(scaled, x, y) * tile(inverse, x, y) + ratio * tile(field, x, y))
            return carry

        lax.fori_loop(0, nx, turn, 0)
    pressure[...] = mine
    residual[...] = tile(scaled, my_x, my_y) - step_size * tile(image, my_x, my_y)


def tracers_kernel(
    fold_map, tracer, east_vel, north_vel, diffusion, mixing, count, from_east, from_west, near, far, extra,
    mixed,
    north_rows, south_rows, factors,
):
    lane, sub = lanes(), sublanes()
    levels = count[...]
    group = pl.program_id(0)

    @pl.when(group == 0)
    def _():
        halo_rows(fold_map, near, far, extra, north_rows, south_rows)
        c_prev = jnp.zeros((ROWS, COLS), jnp.float32)
        a_prev = jnp.zeros((ROWS, COLS), jnp.float32)
        for k in range(LEVELS):
            wet = jnp.where(k < levels, 1.0, 0.0)
            u, v, spread = 0.5 * wet * east_vel[k], 0.5 * wet * north_vel[k], wet * diffusion[k]
            a = jnp.where(k + 1 < levels, mixing[k], 0.0)
            inverse = 1.0 / (1.0 + a_prev + a + a_prev * c_prev)
            c_prev = -a * inverse
            factors[0, k] = 1.0 - 4.0 * spread
            factors[1, k] = spread - u
            factors[2, k] = spread + u
            factors[3, k] = spread - v
            factors[4, k] = spread + v
            factors[5, k] = inverse
            factors[6, k] = a_prev
            factors[7, k] = c_prev
            a_prev = a

    row = pl.multiple_of(group * ROWS, ROWS)
    columns_east = from_east[pl.ds(row, ROWS), :]
    columns_west = from_west[pl.ds(row, ROWS), :]
    r_prev = [jnp.zeros((ROWS, COLS), jnp.float32)] * GROUP
    for k in range(LEVELS):
        centre, to_e, to_w, to_n, to_s, inverse, above = (factors[j, k] for j in range(7))
        wet = k < levels
        for t in range(GROUP):
            cell = jnp.where(wet, tracer[t, k], 0.0)
            at = t * LEVELS + k
            halo_row = group * (GROUP * LEVELS) + at
            east = east_of(cell, roll(columns_east, -at, 1), lane)
            west = west_of(cell, roll(columns_west, COLS - 1 - at, 1), lane)
            north = north_of(cell, north_rows[pl.ds(halo_row, 1), :], sub)
            south = south_of(cell, south_rows[pl.ds(halo_row, 1), :], sub)
            explicit = centre * cell + to_e * east + to_w * west + to_n * north + to_s * south
            r_prev[t] = (explicit + above * r_prev[t]) * inverse
            mixed[t, k] = r_prev[t]
    x_next = r_prev
    for k in range(LEVELS - 2, -1, -1):
        below = factors[7, k]
        for t in range(GROUP):
            x_next[t] = mixed[t, k] - below * x_next[t]
            mixed[t, k] = x_next[t]


def shards(sizes, tracer, east_vel, north_vel, diffusion, mixing, level_count, fold_map, surface_term):
    nx, ny = sizes
    f32 = jnp.float32
    grid_rows = nx * ny * ROWS

    def device(x, y):
        return (x % nx) * ny + y

    def kernel(body, **rest):
        return pl.pallas_call(body, compiler_params=params(), **rest)

    def shape(*dims):
        return jax.ShapeDtypeStruct(dims, f32)

    def vmem(*dims):
        return pltpu.VMEM(dims, f32)

    def all_of(array):
        return pl.BlockSpec(array.shape, lambda i: (0,) * array.ndim)

    smem = pl.BlockSpec(memory_space=pltpu.SMEM)
    hbm = pl.BlockSpec(memory_space=pltpu.HBM)
    fields = (east_vel, north_vel, diffusion, mixing)
    flat = tracer.reshape(EDGE * ROWS, COLS)

    to_west, to_east, near, far, shared = kernel(
        pack_kernel,
        out_shape=(
            shape(GROUPS * ROWS, COLS),
            shape(GROUPS * ROWS, COLS),
            shape(EDGE, COLS),
            shape(EDGE, COLS),
            shape(nx * ny, 2 * ROWS, COLS),
        ),
        in_specs=[hbm] * 3,
        out_specs=(whole(),) * 5,
        scratch_shapes=[
            vmem(EDGE * ROWS, COLS),
            pltpu.VMEM((ROWS, COLS), jnp.int32),
            vmem(ROWS, COLS),
            pltpu.SemaphoreType.DMA((GROUPS + 2,)),
        ],
        name="pack",
    )(flat, level_count, surface_term)

    from_east = lax.ppermute(to_west, BOTH, [(device(x + 1, y), device(x, y)) for x in range(nx) for y in range(ny)])
    from_west = lax.ppermute(to_east, BOTH, [(device(x - 1, y), device(x, y)) for x in range(nx) for y in range(ny)])
    near = lax.ppermute(near, BOTH, [(device(x, y ^ 1), device(x, y)) for x in range(nx) for y in range(ny)])
    inner = [(device(x, y + 1 if y % 2 else y - 1), device(x, y)) for x in range(nx) for y in range(1, ny - 1)]
    shared = lax.all_to_all(shared, BOTH, 0, 0)

    def across(turn):
        return [(device(turn - x, ny - 1), device(x, ny - 1)) for x in range(nx)]

    def exchange(block, rows):
        turns = ((block - 1) % nx, block)
        even, odd = turns if turns[0] % 2 == 0 else turns[::-1]
        return lax.ppermute(rows, BOTH, inner + across(even)), lax.ppermute(rows, BOTH, across(odd))

    block = pole_of(fold_map) >> (COLS.bit_length() - 1)
    far, extra = lax.switch(block, [functools.partial(exchange, i) for i in range(nx)], far)

    pair = pl.BlockSpec((2, LEVELS, ROWS, COLS), lambda i: (0, 0, 0, 0))
    two = pl.BlockSpec((2 * LEVELS, COLS), lambda i: (0, 0))
    tile = pl.BlockSpec((ROWS, COLS), lambda i: (0, 0))
    rhs = kernel(
        right_side_kernel,
        grid=(1,),
        out_shape=shape(nx * ny, ROWS, COLS),
        in_specs=[smem, pair] + [all_of(array) for array in (*fields, level_count)] + [tile, tile, two, two, two],
        out_specs=pl.BlockSpec((nx * ny, ROWS, COLS), lambda i: (0, 0, 0)),
        scratch_shapes=[vmem(2 * LEVELS, COLS), vmem(2 * LEVELS, COLS)],
        name="right_side",
    )(fold_map, tracer, *fields, level_count, from_east, from_west, near, far, extra)
    rhs = lax.all_to_all(rhs, BOTH, 0, 0).reshape(grid_rows, COLS)

    batch = pl.BlockSpec((GROUP, LEVELS, ROWS, COLS), lambda i: (i, 0, 0, 0))
    edge = pl.BlockSpec((EDGE, COLS), lambda i: (0, 0))
    tiles = pl.BlockSpec((GROUPS * ROWS, COLS), lambda i: (0, 0))
    mixed = kernel(
        tracers_kernel,
        grid=(GROUPS,),
        out_shape=shape(TRACERS, LEVELS, ROWS, COLS),
        in_specs=[smem, batch] + [all_of(array) for array in (*fields, level_count)] + [tiles, tiles, edge, edge, edge],
        out_specs=batch,
        scratch_shapes=[vmem(EDGE, COLS), vmem(EDGE, COLS), vmem(8, LEVELS, ROWS, COLS)],
        name="tracers",
    )(fold_map, tracer, *fields, level_count, from_east, from_west, near, far, extra)

    pressure, residual = kernel(
        gradients_kernel,
        out_shape=(shape(ROWS, COLS), shape(ROWS, COLS)),
        in_specs=[smem, whole(), whole()],
        out_specs=(whole(), whole()),
        scratch_shapes=[vmem(grid_rows, COLS) for _ in range(13)] + [vmem(nx, COLS)],
        name="gradients",
    )(fold_map, rhs, shared)
    return mixed, pressure, residual


def solution(mesh):
    in_specs = (
        P(None, None, "gy", "gx"),
        P(None, "gy", "gx"),
        P(None, "gy", "gx"),
        P(None, "gy", "gx"),
        P(None, "gy", "gx"),
        P("gy", "gx"),
        P(),
        P("gy", "gx"),
    )
    out_specs = (P(None, None, "gy", "gx"), P("gy", "gx"), P("gy", "gx"))
    body = functools.partial(shards, (mesh.shape["gx"], mesh.shape["gy"]))
    return jax.shard_map(body, mesh=mesh, in_specs=in_specs, out_specs=out_specs, check_vma=False)
```

time: 734 us -> 90.1 us (0.12)
  blocking collectives: 524 us -> 25.7 us
  waiting for transfers between devices: 60.7 us -> 18.5 us
  starting transfers between devices: 53.3 us -> 16.9 us
  local copies, waits for them, and re-layouts: 40.6 us -> 7.75 us
  other arithmetic: 28.9 us -> 0 us
  between operations: 24.7 us -> 1.4 us
  Pallas kernels: 0 us -> 19.2 us
    psum x7 -> x0, blocking collectives: 451 us -> none  [the longest x4 255 us: residual_energy(): return lax.psum(jnp.sum(resid * scaled_now), ('gx', 'gy'))]
    all_gather x5 -> x0, blocking collectives: 72.8 us -> none  [extend(): whole_row = lax.all_gather(top_row, 'gx', axis=2, tiled=True)]
    ppermute x24 -> x5, starting transfers between devices: 53.3 us -> 12.3 us  [the longest x1 6.29 us: shards(): lax.ppermute(to_west, BOTH, [(device(x + 1, y), device(x, y)) for x in ra...]
    ppermute x24 -> x5, waiting for transfers between devices: 41.7 us -> 3.45 us  [the longest x1 3.44 us: exchange(): lax.ppermute(rows, BOTH, inner + across(even))]
    all_to_all x0 -> x1, blocking collectives: none -> 25.7 us  [shards(): rhs = lax.all_to_all(rhs, BOTH, 0, 0).reshape(grid_rows, COLS)]
    pallas_call x0 -> x4, Pallas kernels: none -> 19.2 us  [the longest x1 12.2 us: shards(): kernel(gradients_kernel, out_shape=(shape(ROWS, COLS), shape(ROWS, COLS))...]
    all_gather x1 -> x0, waiting for transfers between devices: 18.9 us -> none  [extend(): whole_row = lax.all_gather(top_row, 'gx', axis=2, tiled=True)]
    gather x7 -> x0, local copies, waits for them, and re-layouts: 16.5 us -> none  [extend(): folded = jnp.take(whole_row, partner, axis=2)]
  transfers between devices with their start and end apart: 25 -> 6, of which waited for: 21 -> 2; matrix products, arithmetic and copies ran while one was open for 6% -> 1% of each run, Pallas kernels for 0% -> 5%
where the time goes in v2:
time: 90.1 us; the launch traced here: 89.5 us
  blocking collectives  25.7 us (29%)
  Pallas kernels  19.2 us (21%)
  waiting for transfers between devices  18.5 us (21%)
  starting transfers between devices  16.9 us (19%)
  local copies, waits for them, and re-layouts  7.75 us (9%)
  between operations  1.4 us (2%)
    all_to_all x1, blocking collectives, shards(): rhs = lax.all_to_all(rhs, BOTH, 0, 0).reshape(grid_rows, COLS)  25.7 us
    all_to_all x1, waiting for transfers between devices, shards(): shared = lax.all_to_all(shared, BOTH, 0, 0)  15 us
    pallas_call x1, Pallas kernels, shards(): kernel(gradients_kernel, out_shape=(shape(ROWS, COLS), shape(ROWS, COLS))...  12.2 us
    unnamed x30, local copies, waits for them, and re-layouts  7.23 us
    ppermute x1, starting transfers between devices, shards(): lax.ppermute(to_west, BOTH, [(device(x + 1, y), device(x, y)) for x in ra...  6.29 us
    all_to_all x1, starting transfers between devices, shards(): shared = lax.all_to_all(shared, BOTH, 0, 0)  4.52 us
    pallas_call x1, Pallas kernels, shards(): kernel(tracers_kernel, grid=(GROUPS,), out_shape=shape(TRACERS, LEVELS, R...  4.35 us
    ppermute x1, waiting for transfers between devices, exchange(): lax.ppermute(rows, BOTH, inner + across(even))  3.44 us
  transfers between devices with their start and end apart: 6, of which 2 were waited for; matrix products, arithmetic and copies ran while one was open for 1% of the time, Pallas kernels for 5%

profile of v2, /device:TPU:1, one launch (start us, length us, event | category | flops | bytes accessed | tf_op | source)
XLA Modules:
  0.0 89.5 jit_solution(10255944671919357805)
XLA Ops:
  0.6 1.3 %copy-done = f32[16,20,8,128]{3,2,1,0:T(8,128)S(1)} copy-done((f32[16,20,8,128]{3,2,1,0:T(8,128)S(1)}, f32[16,20,8,128]{3,2,1,0:T(8,128)}, u32[]{:S(2)}) %copy-start) | copy-done | bytes 1310744
  2.0 0.7 copy-done.12
  2.6 0.7 copy-done.14
  3.3 1.5 %pack.1 = (f32[32,128]{1,0:T(8,128)S(1)}, f32[32,128]{1,0:T(8,128)S(1)}, f32[320,128]{1,0:T(8,128)S(1)}, f32[320,128]{1,0:T(8,128)S(1)}, f32[128,16,128]{2,1,0:T(8,128)S(1)}) custom-call(f32[2560,128]{1,0:T(8,128)S(1)} %bitcast.3, s32[8,128]{1,0:T(8,128)S(1)} %copy-done.12, f32[8,128]{1,0:T(8,128)S(1)} %copy-done.14), custom_call_target="tpu_custom_call" | custom-call | tf_op jit(solution)/shard_map/pack/pallas_call | solution.py:447
  4.9 1.0 %copy-done.2 = f32[128,16,128]{2,1,0:T(8,128)} copy-done((f32[128,16,128]{2,1,0:T(8,128)}, f32[128,16,128]{2,1,0:T(8,128)S(1)}, u32[]{:S(2)}) %copy-start.2) | copy-done | bytes 1048600
  5.8 1.4 %collective-permute-start.34 = (f32[320,128]{1,0:T(8,128)S(1)}, f32[320,128]{1,0:T(8,128)S(1)}, u32[]{:S(2)}, u32[]{:S(2)}) collective-permute-start(f32[320,128]{1,0:T(8,128)S(1)} %get-tuple-element.30), channel_id=1, source_target_pairs={{1,0},{0,1},{3,2},{2,3},{5,4},{4,5},{7,6},{6,7},{9,8},{8,9},{11,10... | collective-permute-start | bytes 491528 | tf_op jit(solution)/shard_map/ppermute | solution.py:469
  7.3 6.3 %collective-permute-start.32 = (f32[32,128]{1,0:T(8,128)S(1)}, f32[32,128]{1,0:T(8,128)S(1)}, u32[]{:S(2)}, u32[]{:S(2)}) collective-permute-start(f32[32,128]{1,0:T(8,128)S(1)} %get-tuple-element.28), channel_id=1, source_target_pairs={{8,0},{9,1},{10,2},{11,3},{12,4},{13,5},{14,6},{15,7},{16,8},{17,9... | collective-permute-start | bytes 49160 | tf_op jit(solution)/shard_map/ppermute | solution.py:467
  13.6 0.5 slice.3
  14.7 8.1 %conditional.1 = (f32[320,128]{1,0:T(8,128)}, f32[320,128]{1,0:T(8,128)}) conditional(s32[]{:T(128)} %bitcast.1, f32[320,128]{1,0:T(8,128)S(1)} %get-tuple-element.31, f32[320,128]{1,0:T(8,128)S(1)} %get-tuple-element.31, f32[320,128]{1,0:T(8,128)S(1)} %get-tuple-element.31, ...), branch_computations={%region_0.0_spmd, %region_1.0_spmd, %region_2.0_spmd, %region_3.0_... | conditional | bytes 1310816 | solution.py:482
  14.8 1.4 %collective-permute-start.13 = (f32[320,128]{1,0:T(8,128)S(1)}, f32[320,128]{1,0:T(8,128)}, u32[]{:S(2)}, u32[]{:S(2)}) collective-permute-start(f32[320,128]{1,0:T(8,128)S(1)} %param.6), channel_id=1, source_target_pairs={{47,7},{39,15},{31,23},{23,31},{15,39},{7,47},{127,55},{119,63},{1... | collective-permute-start | bytes 491528 | tf_op jit(solution)/shard_map/cond/branch_6_fun/ppermute | solution.py:479
  16.1 3.3 %collective-permute-start.12 = (f32[320,128]{1,0:T(8,128)S(1)}, f32[320,128]{1,0:T(8,128)}, u32[]{:S(2)}, u32[]{:S(2)}) collective-permute-start(f32[320,128]{1,0:T(8,128)S(1)} %param.6), channel_id=1, source_target_pairs={{2,1},{1,2},{4,3},{3,4},{6,5},{5,6},{10,9},{9,10},{12,11},{11,12},... | collective-permute-start | bytes 491528 | tf_op jit(solution)/shard_map/cond/branch_6_fun/ppermute | solution.py:479
  19.4 0.0 collective-permute-done.13
  19.4 3.4 %collective-permute-done.12 = f32[320,128]{1,0:T(8,128)} collective-permute-done((f32[320,128]{1,0:T(8,128)S(1)}, f32[320,128]{1,0:T(8,128)}, u32[]{:S(2)}, u32[]{:S(2)}) %collective-permute-start.12) | collective-permute-done | bytes 163872 | tf_op jit(solution)/shard_map/cond/branch_6_fun/ppermute | solution.py:479
  22.9 0.0 copy-start.3
  22.9 0.9 copy-done.3
  23.8 0.9 copy-done.5
  24.7 0.9 copy-done.7
  25.5 0.9 copy-done.9
  26.4 1.2 %right_side.1 = f32[128,8,128]{2,1,0:T(8,128)S(1)} custom-call(s32[2048]{0:T(1024)S(1)} %copy-done.11, f32[16,20,8,128]{3,2,1,0:T(8,128)S(1)} %copy-done.1, f32[20,8,128]{2,1,0:T(8,128)S(1)} %copy-done.3, f32[20,8,128]{2,1,0:T(8,128)S(1)} %copy-done.5, f32[20,8,128]{2,1,0:T(8,128)S(1)} %copy-done.7, f32[20,8,128]{2,1,0:T(8,128)S(1)} %copy-done.9, ...), custom_call_target="tpu_custom_call" | custom-call | tf_op jit(solution)/shard_map/right_side/pallas_call | solution.py:487
  27.6 25.7 %all_to_all.10 = f32[128,8,128]{2,1,0:T(8,128)S(1)} all-to-all(f32[128,8,128]{2,1,0:T(8,128)S(1)} %right_side.1), channel_id=1, replica_groups=mesh['gx'=16,'gy'=8] {'gx','gy'}, dimensions={0} | all-to-all | bytes 1048576 | tf_op jit(solution)/shard_map/all_to_all | solution.py:496
  53.4 4.5 %all-to-all-start.1 = ((f32[128,16,128]{2,1,0:T(8,128)}), f32[128,16,128]{2,1,0:T(8,128)S(1)}, u32[]{:S(2)}, u32[]{:S(2)}) async-start(f32[128,16,128]{2,1,0:T(8,128)} %copy-done.2), calls=%async_computation.1 | async-start | bytes 2097152 | tf_op jit(solution)/shard_map/all_to_all | solution.py:471
  57.9 4.4 %tracers.1 = f32[16,20,8,128]{3,2,1,0:T(8,128)} custom-call(s32[2048]{0:T(1024)S(1)} %copy-done.11, f32[16,20,8,128]{3,2,1,0:T(8,128)S(1)} %copy-done.1, f32[20,8,128]{2,1,0:T(8,128)S(1)} %copy-done.4, f32[20,8,128]{2,1,0:T(8,128)S(1)} %copy-done.6, f32[20,8,128]{2,1,0:T(8,128)S(1)} %copy-done.8, f32[20,8,128]{2,1,0:T(8,128)S(1)} %copy-done.10, ...), custom_call_target="tpu_custom_call" | custom-call | tf_op jit(solution)/shard_map/tracers/pallas_call | solution.py:501
  62.3 15.0 %all-to-all-done.1.shared = f32[128,16,128]{2,1,0:T(8,128)S(1)} async-done(((f32[128,16,128]{2,1,0:T(8,128)}), f32[128,16,128]{2,1,0:T(8,128)S(1)}, u32[]{:S(2)}, u32[]{:S(2)}) %all-to-all-start.1) | async-done | bytes 1048608 | tf_op jit(solution)/shard_map/all_to_all | solution.py:471
  77.3 12.2 %gradients.1 = (f32[8,128]{1,0:T(8,128)}, f32[8,128]{1,0:T(8,128)}) custom-call(s32[2048]{0:T(1024)S(1)} %copy-done.11, f32[1024,128]{1,0:T(8,128)S(1)} %bitcast.4, f32[128,16,128]{2,1,0:T(8,128)S(1)} %all-to-all-done.1.shared), custom_call_target="tpu_custom_call" | custom-call | tf_op jit(solution)/shard_map/gradients/pallas_call | solution.py:511
  (25 shorter events, 0.0 us)
Async XLA Ops:
  0.6 1.3 %copy-start = (f32[16,20,8,128]{3,2,1,0:T(8,128)S(1)}, f32[16,20,8,128]{3,2,1,0:T(8,128)}, u32[]{:S(2)}) copy-start(f32[16,20,8,128]{3,2,1,0:T(8,128)} %tracer.3) | copy-start | bytes 3932164
  1.9 0.7 copy-start.12
  2.6 0.7 copy-start.14
  3.3 10.2 %copy-start.11 = (s32[2048]{0:T(1024)S(1)}, s32[2048]{0:T(1024)}, u32[]{:S(2)}) copy-start(s32[2048]{0:T(1024)} %fold_map.5) | copy-start | bytes 24580
  3.3 19.5 %copy-start.1 = (f32[16,20,8,128]{3,2,1,0:T(8,128)S(1)}, f32[16,20,8,128]{3,2,1,0:T(8,128)}, u32[]{:S(2)}) copy-start(f32[16,20,8,128]{3,2,1,0:T(8,128)} %tracer.3) | copy-start | bytes 3932164
  3.3 19.5 %copy-start.13 = (s32[8,128]{1,0:T(8,128)S(1)}, s32[8,128]{1,0:T(8,128)}, u32[]{:S(2)}) copy-start(s32[8,128]{1,0:T(8,128)} %count.5) | copy-start | bytes 12292
  4.9 1.0 %copy-start.2 = (f32[128,16,128]{2,1,0:T(8,128)}, f32[128,16,128]{2,1,0:T(8,128)S(1)}, u32[]{:S(2)}) copy-start(f32[128,16,128]{2,1,0:T(8,128)S(1)} %get-tuple-element.34) | copy-start | bytes 3145732
  5.8 17.0 %collective-permute-start.34 = (f32[320,128]{1,0:T(8,128)S(1)}, f32[320,128]{1,0:T(8,128)S(1)}, u32[]{:S(2)}, u32[]{:S(2)}) collective-permute-start(f32[320,128]{1,0:T(8,128)S(1)} %get-tuple-element.30), channel_id=1, source_target_pairs={{1,0},{0,1},{3,2},{2,3},{5,4},{4,5},{7,6},{6,7},{9,8},{8,9},{11,10... | collective-permute-start | bytes 491528 | tf_op jit(solution)/shard_map/ppermute | solution.py:469
  7.3 15.6 %collective-permute-start.32 = (f32[32,128]{1,0:T(8,128)S(1)}, f32[32,128]{1,0:T(8,128)S(1)}, u32[]{:S(2)}, u32[]{:S(2)}) collective-permute-start(f32[32,128]{1,0:T(8,128)S(1)} %get-tuple-element.28), channel_id=1, source_target_pairs={{8,0},{9,1},{10,2},{11,3},{12,4},{13,5},{14,6},{15,7},{16,8},{17,9... | collective-permute-start | bytes 49160 | tf_op jit(solution)/shard_map/ppermute | solution.py:467
  13.6 9.3 %collective-permute-start.33 = (f32[32,128]{1,0:T(8,128)S(1)}, f32[32,128]{1,0:T(8,128)S(1)}, u32[]{:S(2)}, u32[]{:S(2)}) collective-permute-start(f32[32,128]{1,0:T(8,128)S(1)} %get-tuple-element.29), channel_id=1, source_target_pairs={{120,0},{121,1},{122,2},{123,3},{124,4},{125,5},{126,6},{127,7},{0... | collective-permute-start | bytes 49160 | tf_op jit(solution)/shard_map/ppermute | solution.py:468
  14.8 4.6 %collective-permute-start.13 = (f32[320,128]{1,0:T(8,128)S(1)}, f32[320,128]{1,0:T(8,128)}, u32[]{:S(2)}, u32[]{:S(2)}) collective-permute-start(f32[320,128]{1,0:T(8,128)S(1)} %param.6), channel_id=1, source_target_pairs={{47,7},{39,15},{31,23},{23,31},{15,39},{7,47},{127,55},{119,63},{1... | collective-permute-start | bytes 491528 | tf_op jit(solution)/shard_map/cond/branch_6_fun/ppermute | solution.py:479
  16.1 6.7 %collective-permute-start.12 = (f32[320,128]{1,0:T(8,128)S(1)}, f32[320,128]{1,0:T(8,128)}, u32[]{:S(2)}, u32[]{:S(2)}) collective-permute-start(f32[320,128]{1,0:T(8,128)S(1)} %param.6), channel_id=1, source_target_pairs={{2,1},{1,2},{4,3},{3,4},{6,5},{5,6},{10,9},{9,10},{12,11},{11,12},... | collective-permute-start | bytes 491528 | tf_op jit(solution)/shard_map/cond/branch_6_fun/ppermute | solution.py:479
  22.9 0.9 copy-start.3
  23.8 0.9 copy-start.5
  24.7 0.9 copy-start.7
  25.5 0.9 copy-start.9
  53.3 4.5 %copy-start.4 = (f32[20,8,128]{2,1,0:T(8,128)S(1)}, f32[20,8,128]{2,1,0:T(8,128)}, u32[]{:S(2)}) copy-start(f32[20,8,128]{2,1,0:T(8,128)} %east_vel.3) | copy-start | bytes 245764
  53.3 4.5 %copy-start.6 = (f32[20,8,128]{2,1,0:T(8,128)S(1)}, f32[20,8,128]{2,1,0:T(8,128)}, u32[]{:S(2)}) copy-start(f32[20,8,128]{2,1,0:T(8,128)} %north_vel.3) | copy-start | bytes 245764
  53.3 4.6 %copy-start.8 = (f32[20,8,128]{2,1,0:T(8,128)S(1)}, f32[20,8,128]{2,1,0:T(8,128)}, u32[]{:S(2)}) copy-start(f32[20,8,128]{2,1,0:T(8,128)} %diffusion.3) | copy-start | bytes 245764
  53.3 4.6 %copy-start.10 = (f32[20,8,128]{2,1,0:T(8,128)S(1)}, f32[20,8,128]{2,1,0:T(8,128)}, u32[]{:S(2)}) copy-start(f32[20,8,128]{2,1,0:T(8,128)} %mixing.3) | copy-start | bytes 245764
  53.4 23.9 %all-to-all-start.1 = ((f32[128,16,128]{2,1,0:T(8,128)}), f32[128,16,128]{2,1,0:T(8,128)S(1)}, u32[]{:S(2)}, u32[]{:S(2)}) async-start(f32[128,16,128]{2,1,0:T(8,128)} %copy-done.2), calls=%async_computation.1 | async-start | bytes 2097152 | tf_op jit(solution)/shard_map/all_to_all | solution.py:471
